TPU v7x, 256 devices: a whole 4x4x8 slice. The times are simulated.
256 devices in a mesh: dp: 16 (over x_hi, z), tensor: 16 (over x_lo, y, core).
Axes of the slice: x: 4 (x_hi: 2, x_lo: 2; x = x_hi * 2 + x_lo), y: 4, z: 8, core: 2. Of those that a mesh axis runs over, the one named last changes fastest.
Arguments:
- hidden: bfloat16 [32, 128, 28672], P('dp', None, 'tensor'), may hold values from -6 to 6
- out_grad: bfloat16 [32, 128, 8192], P('dp'), may hold values from -6 to 6
- w_down: bfloat16 [28672, 8192], P('tensor', 'dp'), may hold values from -0.0625 to 0.0625
- proj_in: bfloat16 [28672, 64], P('tensor'), may hold values from -0.03125 to 0.03125
- proj_out: bfloat16 [8192, 64], replicated, may hold values from -0.0625 to 0.0625
- queries: float32 [2048, 4096], P(('dp', 'tensor')), may hold values from -6 to 6
Outputs:
- back_grad: bfloat16 [32, 128, 28672], P('dp', None, 'tensor')
- scores: float32 [32, 2048], P(None, ('dp', 'tensor'))
All inputs are finite; a program needn't handle non-finite values.
Results may differ from a plain program's by a relative error of at most 0.001.
Values may be sent and summed in bfloat16 or wider, within the bound.
No kernel may reach another device: no remote copies, remote signals or barrier semaphores. Data moves between devices by JAX's collectives and lax.ppermute only.
A program may use at most 128 MiB of HBM per device.

v0:
```python
import math

import jax
import jax.numpy as jnp
from jax import lax
from jax.sharding import PartitionSpec as P


def per_device(hidden, out_grad, w_down, proj_in, proj_out, queries):
    ex_dev, seq_len, ff_dev = hidden.shape
    model_width = out_grad.shape[2]
    tok_rows = ex_dev * seq_len
    proj_rank = proj_in.shape[1]
    grads_flat = out_grad.reshape(tok_rows, model_width)
    hidden_flat = hidden.reshape(tok_rows, ff_dev)
    inputs_part = jnp.dot(hidden_flat, proj_in, preferred_element_type=jnp.float32)
    inputs_proj = lax.psum(inputs_part, "tensor")
    grads_proj = jnp.dot(grads_flat, proj_out, preferred_element_type=jnp.float32)
    features = jnp.einsum(
        "esi,esj->eij",
        inputs_proj.reshape(ex_dev, seq_len, proj_rank),
        grads_proj.reshape(ex_dev, seq_len, proj_rank),
        precision=lax.Precision.HIGHEST,
    )
    features = features.reshape(ex_dev, proj_rank * proj_rank)
    score_scale = 1.0 / (proj_rank * math.sqrt(seq_len))
    scores = (
        jnp.dot(
            lax.all_gather(features, "dp", axis=0, tiled=True),
            queries.T,
            precision=lax.Precision.HIGHEST,
        )
        * score_scale
    )
    back_sum = lax.dot_general(
        grads_flat,
        lax.all_gather(w_down, "dp", axis=1, tiled=True),
        (((1,), (1,)), ((), ())),
        preferred_element_type=jnp.float32,
    )
    back_grad = back_sum.astype(jnp.bfloat16).reshape(ex_dev, seq_len, ff_dev)
    return (back_grad, scores)


def solution(mesh):
    return jax.shard_map(
        per_device,
        mesh=mesh,
        in_specs=(
            P("dp", None, "tensor"),
            P("dp", None, None),
            P("tensor", "dp"),
            P("tensor", None),
            P(),
            P(("dp", "tensor"), None),
        ),
        out_specs=(P("dp", None, "tensor"), P(None, ("dp", "tensor"))),
        check_vma=False,
    )
```

profile of v0, /device:TPU:6, one launch (start us, length us, event | category | flops | bytes accessed | tf_op | source)
XLA Modules:
  0.0 421.9 jit_solution(7946261867376743012)
XLA Ops:
  8.0 0.0 copy-start
  8.0 0.0 all-reduce.2.cloned.1.call-start
  8.1 1.7 convolution_bitcast_fusion
  9.8 0.6 copy.12
  10.4 0.0 all-reduce.2.cloned.1.call-update
  10.4 0.0 copy-start.1
  10.4 0.0 all-gather.3.cloned.1.call-start
  10.5 0.5 all-gather.3.cloned.1.call-update
  11.0 0.0 copy-done
  11.0 3.6 fusion
  14.6 282.1 %all-reduce.2.cloned.1.call-done = f32[2,128,64]{1,2,0:T(8,128)} async-done(((f32[2,128,64]{1,2,0:T(8,128)}), f32[2,128,64]{1,2,0:T(8,128)}) %all-reduce.2.cloned.1.call-update) | async-done | bytes 65552 | tf_op jit(solution)/shard_map/psum | solution.py:17
  296.7 1.1 fusion.2
  297.8 0.1 reshape.27
  297.9 47.9 %all-gather = f32[16,2,4096]{2,1,0:T(2,128)S(1)} all-gather(f32[1,2,4096]{2,1,0:T(2,128)S(1)} %reshape.27), channel_id=1, replica_groups=mesh['dp'=16,'tensor'=16] {'dp'}, dimensions={0}, use_global_device_ids=true | all-gather | bytes 557056 | tf_op jit(solution)/shard_map/all_gather | solution.py:29
  345.7 0.4 reshape.28
  346.1 0.0 copy-done.1
  346.1 1.1 convolution_multiply_fusion
  347.2 52.2 %all-gather.3.cloned.1.call-done = bf16[1792,8192]{1,0:T(8,128)(2,1)} async-done(((bf16[1792,512]{1,0:T(8,128)(2,1)}), bf16[1792,8192]{1,0:T(8,128)(2,1)}) %all-gather.3.cloned.1.call-update) | async-done | bytes 29360144 | tf_op jit(solution)/shard_map/all_gather | solution.py:37
  399.5 15.0 %convolution_convert_fusion = bf16[256,1792]{1,0:T(8,128)(2,1)} fusion(bf16[256,8192]{1,0:T(8,128)(2,1)} %bitcast.20, bf16[1792,8192]{1,0:T(8,128)(2,1)} %all-gather.3.cloned.1.call-done), kind=kOutput, calls=%fused_computation | convolution fusion | flops 7516651520 | bytes 34471936 | tf_op jit(solution)/shard_map/dot_general | solution.py:35
Async XLA Ops:
  8.0 3.0 copy-start
  8.0 288.7 %all-reduce.2.cloned.1.call-start = ((), (), s32[]{:S(2)}) async-start(), calls=%async_computation.1 | async-start | bytes 131072 | tf_op jit(solution)/shard_map/psum | solution.py:17
  10.4 335.7 %copy-start.1 = (f32[8,4096]{1,0:T(8,128)S(1)}, f32[8,4096]{1,0:T(8,128)}, u32[]{:S(2)}) copy-start(f32[8,4096]{1,0:T(8,128)} %param.11) | copy-start | bytes 393220
  10.4 389.0 %all-gather.3.cloned.1.call-start = ((), (), s32[]{:S(2)}) async-start(), calls=%async_computation | async-start | bytes 31195136 | tf_op jit(solution)/shard_map/all_gather | solution.py:37
Sparse Core Ops, SparseCore 0:
  12.0 284.6 all-reduce.1
Sparse Core Ops, SparseCore 1:
  13.4 386.0 all-gather.2
where the time goes:
time: 424 us; the launch traced here: 422 us
  waiting for transfers between devices  335 us (79%)
  blocking collectives  47.9 us (11%)
  matrix products  22.5 us (5%)
  between operations  15.5 us (4%)
    psum x1, waiting for transfers between devices, per_device(): inputs_proj = lax.psum(inputs_part, 'tensor')  282 us
    all_gather x1, waiting for transfers between devices, per_device(): lax.all_gather(w_down, 'dp', axis=1, tiled=True)  52.2 us
    all_gather x1, blocking collectives, per_device(): lax.all_gather(features, 'dp', axis=0, tiled=True)  47.9 us
    dot_general x1, matrix products, per_device(): lax.dot_general(grads_flat, lax.all_gather(w_down, 'dp', axis=1, tiled=Tr...  15 us
  transfers between devices with their start and end apart: 2, of which 2 were waited for; matrix products, arithmetic and copies ran while one was open for 1% of the time, Pallas kernels for 0%

commit v1 on v0

v1 whole, which is shorter than its diff:
```python
import functools
import math

import jax
import jax.numpy as jnp
from jax import lax
from jax.experimental import pallas as pl
from jax.experimental.pallas import tpu as pltpu
from jax.sharding import PartitionSpec as P

XH, Z = 2, 8
XL, Y, C = 2, 4, 2
PIECES = Y * C
SPAN = 240.0
PAD = 16
TILE = 128

Z_PERM = {
    r: [(i, (i // Z) * Z + (i + r) % Z) for i in range(XH * Z)] for r in range(-3, 5)
}
X_PERM = [(i, (i + Z) % (XH * Z)) for i in range(XH * Z)]
Y_PERM = {
    r: [(t, (t // PIECES) * PIECES + (t + r * C) % PIECES) for t in range(XL * Y * C)]
    for r in range(1, Y)
}
C_PERM = [(t, t ^ 1) for t in range(XL * Y * C)]
IN_VMEM = pl.BlockSpec(memory_space=pltpu.VMEM)
ANYWHERE = pl.BlockSpec(memory_space=pl.ANY)
LIMIT = 16 * 1024 * 1024


def nt_dot(a, b):
    return lax.dot_general(a, b, (((1,), (1,)), ((), ())), preferred_element_type=jnp.float32)


def encode(out, k, x):
    size = jnp.abs(x)
    top = jnp.maximum(jnp.max(size, axis=0, keepdims=True), 1e-30)
    scale = (top * 1.01).astype(jnp.bfloat16)
    level = size * (SPAN / scale.astype(jnp.float32)) - SPAN / 2
    code = jnp.exp2(level)
    out[k * TILE : (k + 1) * TILE, :] = jnp.where(x < 0, -code, code).astype(jnp.bfloat16)
    return scale


def decode(ref, scales, k):
    code = ref[k * TILE : (k + 1) * TILE, :].astype(jnp.float32)
    unit = scales[k : k + 1, :] * (1.0 / SPAN)
    level = jnp.log(jnp.abs(code)) * (unit * (1.0 / math.log(2.0))) + unit * (SPAN / 2)
    return jnp.where(code < 0, -level, level)


def scales_of(ref):
    rows = ref.shape[0] - PAD
    return ref[rows:, :].astype(jnp.float32)


def add_own(x, w_own, w_other, act):
    half = w_own.shape[1]
    x[...] = nt_dot(w_own[...], act[:, :half]) + nt_dot(w_other[...], act[:, half:])


def stage_kernel(at_r, at_l, part_r, n_in, n_after, mine, other, w_down, w_far, *refs):
    came = refs[:n_in]
    outs = refs[n_in + n_after : n_in + n_after + 2]
    x, acts, far, coming, sems = refs[n_in + n_after + 2 :]
    chunk = w_far.shape[0] // 2
    toks = x.shape[1]
    sides = ((at_r, part_r), (at_l, 1 - part_r))
    copies = []
    for side, (at, part) in enumerate(sides):
        rows = pl.ds(part * chunk, chunk)
        moves = [
            (mine.at[:, at], acts.at[side, :, 0]),
            (other.at[:, at], acts.at[side, :, 1]),
            (w_far.at[rows], far.at[side]),
        ]
        if n_in:
            moves.append((came[side], coming.at[side]))
        started = [pltpu.make_async_copy(src, dst, sems.at[side, k]) for k, (src, dst) in enumerate(moves)]
        for c in started:
            c.start()
        copies.append(started)
    for side, (_, part) in enumerate(sides):
        for c in copies[side]:
            c.wait()
        act = acts[side].reshape(toks, acts.shape[-1])
        add_own(x, w_down.at[pl.ds(part * chunk, chunk)], far.at[side], act)
        if n_in:
            scales = scales_of(coming.at[side])
        new = []
        for k in range(chunk // TILE):
            total = x[k * TILE : (k + 1) * TILE, :]
            if n_in:
                total = total + decode(coming.at[side], scales, k)
            new.append(encode(outs[side], k, total))
        new += [new[-1]] * (PAD - len(new))
        outs[side][chunk:, :] = jnp.concatenate(new, axis=0)


def own_kernel(starts_of, place, own, w_down, w_far, right, left, out):
    chunk = w_far.shape[0] // 2
    act = jnp.concatenate([own[pl.ds(s, n), :] for s, n in starts_of(place[0], place[1])], axis=0)
    for part, ref in ((0, left), (1, right)):
        rows = pl.ds(part * chunk, chunk)
        add_own(out.at[rows], w_down.at[rows], w_far.at[rows], act)
        scales = scales_of(ref)
        for k in range(chunk // TILE):
            at = slice(part * chunk + k * TILE, part * chunk + (k + 1) * TILE)
            out[at, :] = out[at, :] + decode(ref, scales, k)


def last_kernel(starts_of, place, before, right, left, out):
    chunk = before.shape[0] // 2
    starts = starts_of(place[0], place[1])
    for part, ref in ((0, right), (1, left)):
        scales = scales_of(ref)
        for k in range(chunk // TILE):
            row = part * chunk + k * TILE
            total = before[row : row + TILE, :] + decode(ref, scales, k)
            turned = total.T.astype(jnp.bfloat16)
            done = 0
            for s, n in starts:
                out[pl.ds(s, n), row : row + TILE] = turned[done : done + n, :]
                done += n


def pick_kernel(groups, z, planes, _, *outs):
    for offsets, out in zip(groups, outs):
        for k, o in enumerate(offsets):
            out[k] = planes[lax.rem(z[0] + (Z + o), Z)]


def pick(z, planes, groups, after):
    return pl.pallas_call(
        functools.partial(pick_kernel, groups),
        in_specs=[pl.BlockSpec(memory_space=pltpu.SMEM), IN_VMEM, ANYWHERE],
        out_specs=[IN_VMEM] * len(groups),
        out_shape=[jax.ShapeDtypeStruct((len(g), *planes.shape[1:]), planes.dtype) for g in groups],
    )(z.reshape(1).astype(jnp.int32), planes, after)


def cost(rows, toks, depth):
    return pl.CostEstimate(
        flops=2 * rows * toks * depth, bytes_accessed=rows * depth, transcendentals=2 * rows * toks
    )


def stage(at_r, at_l, part_r, mine, other, w_down, w_far, came, after):
    chunk, width = w_far.shape[0] // 2, w_far.shape[1]
    piece, depth = mine.shape[2:]
    toks = piece * PIECES
    coded = jax.ShapeDtypeStruct((chunk + PAD, toks), jnp.bfloat16)
    args = [mine, other, w_down, w_far, *came, *after]
    specs = [ANYWHERE] * len(args)
    specs[2] = IN_VMEM
    return pl.pallas_call(
        functools.partial(stage_kernel, at_r, at_l, part_r, len(came), len(after)),
        in_specs=specs,
        out_specs=[IN_VMEM] * 2,
        out_shape=[coded, coded],
        scratch_shapes=[
            pltpu.VMEM((chunk, toks), jnp.float32),
            pltpu.VMEM((2, Y, C, piece, depth), jnp.bfloat16),
            pltpu.VMEM((2, chunk, width), jnp.bfloat16),
            pltpu.VMEM((2, chunk + PAD, toks), jnp.bfloat16),
            pltpu.SemaphoreType.DMA((2, 4)),
        ],
        compiler_params=pltpu.CompilerParams(vmem_limit_bytes=LIMIT),
        cost_estimate=cost(2 * chunk, toks, depth),
    )(*args)


def starts_of(piece, y, core):
    starts = []
    for r in range(Y):
        for h in range(C):
            c = core if h == 0 else 1 - core
            starts.append((pl.multiple_of((lax.rem(y + r, Y) * C + c) * piece, piece), piece))
    return starts


def finish(place, own, w_down, w_far, early, late):
    toks = own.shape[0]
    rows = w_far.shape[0]
    find = functools.partial(starts_of, toks // PIECES)
    smem = pl.BlockSpec(memory_space=pltpu.SMEM)
    before = pl.pallas_call(
        functools.partial(own_kernel, find),
        in_specs=[smem] + [IN_VMEM] * 5,
        out_specs=IN_VMEM,
        out_shape=jax.ShapeDtypeStruct((rows, toks), jnp.float32),
        compiler_params=pltpu.CompilerParams(vmem_limit_bytes=LIMIT),
        cost_estimate=cost(rows, toks, own.shape[1]),
    )(place, own, w_down, w_far, *early)
    return pl.pallas_call(
        functools.partial(last_kernel, find),
        in_specs=[smem] + [IN_VMEM] * 3,
        out_specs=IN_VMEM,
        out_shape=jax.ShapeDtypeStruct((toks, rows), jnp.bfloat16),
        compiler_params=pltpu.CompilerParams(vmem_limit_bytes=LIMIT),
        cost_estimate=cost(rows, toks, 0),
    )(place, before, *late)


def per_device(hidden, out_grad, w_down, proj_in, proj_out, queries):
    ex_dev, seq_len, ff_dev = hidden.shape
    model_width = out_grad.shape[2]
    toks = ex_dev * seq_len
    proj_rank = proj_in.shape[1]
    width = w_down.shape[1]
    grads_flat = out_grad.reshape(toks, model_width)
    hidden_flat = hidden.reshape(toks, ff_dev)
    dp, t = lax.axis_index("dp"), lax.axis_index("tensor")
    x_hi, z = dp // Z, dp % Z

    w_far = lax.ppermute(w_down, "dp", X_PERM)

    piece_rows = toks // PIECES
    own_rows = lax.dynamic_slice_in_dim(grads_flat, (t % PIECES) * piece_rows, piece_rows, 0)

    def columns(rows_of):
        rows = rows_of.shape[0]
        split = rows_of.reshape(rows, XH, Z, width)
        own = lax.dynamic_index_in_dim(split, x_hi, 1, keepdims=False)
        other = lax.dynamic_index_in_dim(split, 1 - x_hi, 1, keepdims=False)
        return jnp.concatenate([own, other], axis=2).transpose(1, 0, 2)

    rings = [list(range(h * Z, (h + 1) * Z)) for h in range(XH)]
    planes = lax.all_to_all(columns(own_rows), "dp", 0, 0, axis_index_groups=rings, tiled=True)

    inputs_part = jnp.dot(hidden_flat, proj_in, preferred_element_type=jnp.float32)
    grads_proj = jnp.dot(grads_flat, proj_out, preferred_element_type=jnp.float32)
    part = jnp.einsum(
        "esi,esj->eij",
        inputs_part.reshape(ex_dev, seq_len, proj_rank),
        grads_proj.reshape(ex_dev, seq_len, proj_rank),
        precision=lax.Precision.HIGHEST,
    )
    devs_t, devs_d = XL * Y * C, XH * Z
    cols = proj_rank * proj_rank // devs_t
    part = part.reshape(ex_dev, devs_t, cols).transpose(1, 0, 2)
    summed = lax.all_to_all(part, "tensor", 0, 0, tiled=True).sum(axis=0)

    groups = ((4, 3, -3), (2, -2, 1, -1))
    acts = {}
    for offsets, got in zip(groups, pick(z, planes, groups, part)):
        mine = jnp.stack([got] + [lax.ppermute(got, "tensor", Y_PERM[Y - r]) for r in range(1, Y)])
        other = lax.ppermute(mine, "tensor", C_PERM)
        for k, o in enumerate(offsets):
            acts[o] = (k, mine, other)

    over_z = lax.all_to_all(
        jnp.broadcast_to(summed[None], (Z, ex_dev, cols)), "dp", 0, 0, axis_index_groups=rings, tiled=True
    ).reshape(Z * ex_dev, cols)
    over_x = lax.ppermute(over_z, "dp", X_PERM)
    first = x_hi == 0
    over_dp = jnp.concatenate([jnp.where(first, over_z, over_x), jnp.where(first, over_x, over_z)], axis=0)
    features = lax.all_to_all(
        jnp.broadcast_to(over_dp[None], (devs_t, devs_d * ex_dev, cols)), "tensor", 0, 0, tiled=True
    )

    came = {}
    for s in range(7):
        hops = 4 - (s + 1) // 2
        part_r = s % 2
        at_r, mine, other = acts[hops]
        at_l = acts[hops if hops == 4 else -hops][0]
        before = came.get(s - 2, [])
        right, left = stage(
            at_r, at_l, part_r, mine, other, w_down, w_far, before, [over_z if s == 0 else right]
        )
        came[s] = [lax.ppermute(right, "dp", Z_PERM[1]), lax.ppermute(left, "dp", Z_PERM[-1])]
    own_act = jnp.concatenate(
        [
            lax.dynamic_slice_in_dim(grads_flat, (h * Z + z) * width, width, 1)
            for h in (x_hi, 1 - x_hi)
        ],
        axis=1,
    )
    back = finish(jnp.stack([(t // C) % Y, t % C]).astype(jnp.int32), own_act, w_down, w_far, came[5], came[6])
    back_grad = back.reshape(ex_dev, seq_len, ff_dev)

    features = features.transpose(1, 0, 2).reshape(devs_d * ex_dev, proj_rank * proj_rank)
    score_scale = 1.0 / (proj_rank * math.sqrt(seq_len))
    scores = jnp.dot(features, queries.T, precision=lax.Precision.HIGHEST) * score_scale
    return (back_grad, scores)


def solution(mesh):
    return jax.shard_map(
        per_device,
        mesh=mesh,
        in_specs=(
            P("dp", None, "tensor"),
            P("dp", None, None),
            P("tensor", "dp"),
            P("tensor", None),
            P(),
            P(("dp", "tensor"), None),
        ),
        out_specs=(P("dp", None, "tensor"), P(None, ("dp", "tensor"))),
        check_vma=False,
    )
```

time: 424 us -> 166 us (0.39)
  waiting for transfers between devices: 335 us -> 39.3 us
  starting transfers between devices: 0.08 us -> 48.8 us
  Pallas kernels: 0 us -> 42.9 us
  blocking collectives: 47.9 us -> 14.5 us
  matrix products: 22.5 us -> 6.55 us
  between operations: 15.5 us -> 1.01 us
  local copies, waits for them, and re-layouts: 1.11 us -> 6.72 us
  other arithmetic: 0 us -> 5.08 us
    psum x1 -> x0, waiting for transfers between devices: 282 us -> none  [per_device(): inputs_proj = lax.psum(inputs_part, 'tensor')]
    all_gather x1 -> x0, waiting for transfers between devices: 52.2 us -> none  [per_device(): lax.all_gather(w_down, 'dp', axis=1, tiled=True)]
    all_gather x1 -> x0, blocking collectives: 47.9 us -> none  [per_device(): lax.all_gather(features, 'dp', axis=0, tiled=True)]
    pallas_call x0 -> x10, Pallas kernels: none -> 42.9 us  [the longest x7 34.9 us: stage(): pl.pallas_call(functools.partial(stage_kernel, at_r, at_l, part_r, len(ca...]
    ppermute x0 -> x24, starting transfers between devices: none -> 32.2 us  [the longest x7 19.2 us: per_device(): lax.ppermute(left, 'dp', Z_PERM[-1])]
    ppermute x0 -> x24, waiting for transfers between devices: none -> 24.1 us  [the longest x7 13.2 us: per_device(): lax.ppermute(right, 'dp', Z_PERM[1])]
    all_to_all x0 -> x3, starting transfers between devices: none -> 16.6 us  [the longest x1 8.47 us: per_device(): lax.all_to_all(columns(own_rows), 'dp', 0, 0, axis_index_groups=rings, ti...]
    dot_general x3 -> x2, matrix products: 17.2 us -> 1.35 us  [the longest x1 1.12 us: per_device(): jnp.dot(features, queries.T, precision=lax.Precision.HIGHEST) * score_scale]
  transfers between devices with their start and end apart: 2 -> 27, of which waited for: 2 -> 10; matrix products, arithmetic and copies ran while one was open for 1% -> 9% of each run, Pallas kernels for 0% -> 24%
where the time goes in v1:
time: 166 us; the launch traced here: 165 us
  starting transfers between devices  48.8 us (29%)
  Pallas kernels  42.9 us (26%)
  waiting for transfers between devices  39.3 us (24%)
  blocking collectives  14.5 us (9%)
  local copies, waits for them, and re-layouts  6.72 us (4%)
  matrix products  6.55 us (4%)
  other arithmetic  5.08 us (3%)
    pallas_call x7, Pallas kernels, stage(): pl.pallas_call(functools.partial(stage_kernel, at_r, at_l, part_r, len(ca...  34.9 us
    ppermute x7, starting transfers between devices, per_device(): lax.ppermute(left, 'dp', Z_PERM[-1])  19.2 us
    all_to_all x1, blocking collectives, per_device(): summed = lax.all_to_all(part, 'tensor', 0, 0, tiled=True).sum(axis=0)  14.5 us
    ppermute x7, waiting for transfers between devices, per_device(): lax.ppermute(right, 'dp', Z_PERM[1])  13.2 us
    ppermute x6, waiting for transfers between devices, per_device(): lax.ppermute(got, 'tensor', Y_PERM[Y - r])  10.9 us
    all_to_all x1, waiting for transfers between devices, per_device(): lax.all_to_all(columns(own_rows), 'dp', 0, 0, axis_index_groups=rings, ti...  9.82 us
    all_to_all x1, starting transfers between devices, per_device(): lax.all_to_all(columns(own_rows), 'dp', 0, 0, axis_index_groups=rings, ti...  8.47 us
    ppermute x6, starting transfers between devices, per_device(): lax.ppermute(got, 'tensor', Y_PERM[Y - r])  6.69 us
  transfers between devices with their start and end apart: 27, of which 10 were waited for; matrix products, arithmetic and copies ran while one was open for 9% of the time, Pallas kernels for 24%

profile of v1, /device:TPU:6, one launch (start us, length us, event | category | flops | bytes accessed | tf_op | source)
XLA Modules:
  0.0 164.9 jit_solution(15849662530740156149)
XLA Ops:
  0.7 1.2 constant_dynamic-slice_fusion.2
  1.9 0.2 copy.16
  2.2 0.2 copy_bitcast_fusion
  2.3 0.9 maximum_bitcast_fusion
  3.2 8.5 %all-to-all-start = ((bf16[8,32,1024]{2,1,0:T(8,128)(2,1)}), bf16[8,32,1024]{2,1,0:T(8,128)(2,1)S(1)}, u32[]{:S(2)}, u32[]{:S(2)}) async-start(bf16[8,32,1024]{2,1,0:T(8,128)(2,1)} %maximum_bitcast_fusion), calls=%async_computation | async-start | bytes 1048576 | tf_op jit(solution)/shard_map/all_to_all | solution.py:230
  11.7 1.5 collective-permute-start
  13.1 1.6 fusion.2
  14.8 3.6 %fusion = f32[2,128,64]{1,2,0:T(8,128)S(1)} fusion(bf16[2,128,8192]{2,1,0:T(8,128)(2,1)} %param.7, bf16[8192,64]{0,1:T(8,128)(2,1)S(1)} %copy-done), kind=kOutput, calls=%fused_computation.2 | convolution fusion | flops 268435456 | bytes 5308416 | tf_op jit(solution)/shard_map/dot_general | solution.py:233
  18.4 0.2 fusion.4
  18.7 0.6 copy.20
  19.3 9.8 %all-to-all-done.planes = bf16[8,32,1024]{2,1,0:T(8,128)(2,1)S(1)} async-done(((bf16[8,32,1024]{2,1,0:T(8,128)(2,1)}), bf16[8,32,1024]{2,1,0:T(8,128)(2,1)S(1)}, u32[]{:S(2)}, u32[]{:S(2)}) %all-to-all-start) | async-done | bytes 524320 | tf_op jit(solution)/shard_map/all_to_all | solution.py:230
  29.1 0.8 copy-done.2
  29.9 1.9 %shard_map.77 = (bf16[3,32,1024]{2,1,0:T(8,128)(2,1)}, bf16[4,32,1024]{2,1,0:T(8,128)(2,1)}) custom-call(s32[1]{0:T(128)} %bitcast.3.z, bf16[8,32,1024]{2,1,0:T(8,128)(2,1)} %copy-done.2, f32[16,2,256]{2,1,0:T(2,128)} %bitcast.46), custom_call_target="tpu_custom_call" | custom-call | tf_op jit(solution)/shard_map/pallas_call | solution.py:135
  31.8 3.0 %collective-permute-start.5 = (bf16[3,32,1024]{2,1,0:T(8,128)(2,1)}, bf16[3,32,1024]{2,1,0:T(8,128)(2,1)S(1)}, u32[]{:S(2)}, u32[]{:S(2)}) collective-permute-start(bf16[3,32,1024]{2,1,0:T(8,128)(2,1)} %get-tuple-element.19), channel_id=1, source_target_pairs={{0,6},{1,7},{2,0},{3,1},{4,2},{5,3},{6,4},{7,5},{8,14},{9,15},{10,... | collective-permute-start | bytes 589832 | tf_op jit(solution)/shard_map/ppermute | solution.py:248
  34.8 0.6 collective-permute-start.6
  35.4 1.0 collective-permute-start.7
  36.4 7.3 %collective-permute-done.5 = bf16[3,32,1024]{2,1,0:T(8,128)(2,1)S(1)} collective-permute-done((bf16[3,32,1024]{2,1,0:T(8,128)(2,1)}, bf16[3,32,1024]{2,1,0:T(8,128)(2,1)S(1)}, u32[]{:S(2)}, u32[]{:S(2)}) %collective-permute-start.5) | collective-permute-done | bytes 196640 | tf_op jit(solution)/shard_map/ppermute | solution.py:248
  43.7 0.7 collective-permute-done.6
  44.4 2.9 %collective-permute-done.7 = bf16[3,32,1024]{2,1,0:T(8,128)(2,1)S(1)} collective-permute-done((bf16[3,32,1024]{2,1,0:T(8,128)(2,1)}, bf16[3,32,1024]{2,1,0:T(8,128)(2,1)S(1)}, u32[]{:S(2)}, u32[]{:S(2)}) %collective-permute-start.7) | collective-permute-done | bytes 196640 | tf_op jit(solution)/shard_map/ppermute | solution.py:248
  47.3 1.9 %pad_maximum_fusion.1.mine = bf16[4,3,32,1024]{3,2,1,0:T(8,128)(2,1)} fusion(bf16[1,3,32,1024]{3,2,1,0:T(8,128)(2,1)S(1)} %bitcast.54, bf16[1,3,32,1024]{3,2,1,0:T(8,128)(2,1)S(1)} %bitcast.53, bf16[1,3,32,1024]{3,2,1,0:T(8,128)(2,1)S(1)} %bitcast.52, bf16[1,3,32,1024]{3,2,1,0:T(8,128)(2,1)} %bitcast.51), kind=kLoop, calls=%fused_computation.4 | loop fusion | flops 1179648 | bytes 1572864 | tf_op jit(solution)/shard_map/stack | solution.py:248
  49.2 0.1 collective-permute-start.8
  49.3 0.5 collective-permute-start.1
  49.8 0.6 collective-permute-start.2
  50.4 1.0 collective-permute-start.3
  51.4 14.5 %all_to_all.20 = f32[16,2,256]{2,1,0:T(2,128)S(1)} all-to-all(f32[16,2,256]{2,1,0:T(2,128)} %bitcast.47), channel_id=1, replica_groups=mesh['dp'=16,'tensor'=16] {'tensor'}, dimensions={0} | all-to-all | bytes 65536 | tf_op jit(solution)/shard_map/all_to_all | solution.py:243
  66.0 0.6 broadcast_in_dim.4
  66.6 3.3 %all-to-all-start.2 = ((f32[8,2,256]{2,1,0:T(2,128)}), f32[8,2,256]{2,1,0:T(2,128)S(1)}, u32[]{:S(2)}, u32[]{:S(2)}) async-start(f32[8,2,256]{2,1,0:T(2,128)} %broadcast_in_dim.4), calls=%async_computation.2 | async-start | bytes 32768 | tf_op jit(solution)/shard_map/all_to_all | solution.py:253
  69.9 2.2 %pad_maximum_fusion.mine = bf16[4,4,32,1024]{3,2,1,0:T(8,128)(2,1)} fusion(bf16[1,4,32,1024]{3,2,1,0:T(8,128)(2,1)} %bitcast.13, bf16[1,4,32,1024]{3,2,1,0:T(8,128)(2,1)S(1)} %bitcast.50, bf16[1,4,32,1024]{3,2,1,0:T(8,128)(2,1)S(1)} %bitcast.49, bf16[1,4,32,1024]{3,2,1,0:T(8,128)(2,1)} %bitcast.48), kind=kLoop, calls=%fused_computation.1 | loop fusion | flops 1572864 | bytes 2097152 | tf_op jit(solution)/shard_map/stack | solution.py:248
  72.1 0.1 collective-permute-start.4
  72.2 5.4 %all-to-all-done.2 = f32[8,2,256]{2,1,0:T(2,128)S(1)} async-done(((f32[8,2,256]{2,1,0:T(2,128)}), f32[8,2,256]{2,1,0:T(2,128)S(1)}, u32[]{:S(2)}, u32[]{:S(2)}) %all-to-all-start.2) | async-done | bytes 16416 | tf_op jit(solution)/shard_map/all_to_all | solution.py:253
  77.6 3.9 %shard_map.78 = (bf16[912,256]{1,0:T(8,128)(2,1)S(1)}, bf16[912,256]{1,0:T(8,128)(2,1)S(1)}) custom-call(bf16[4,3,32,1024]{3,2,1,0:T(8,128)(2,1)} %pad_maximum_fusion.1.mine, bf16[4,3,32,1024]{3,2,1,0:T(8,128)(2,1)} %collective-permute-done.8.other, bf16[1792,512]{1,0:T(8,128)(2,1)S(1)} %copy-done.1, bf16[1792,512]{1,0:T(8,128)(2,1)} %collective-permute-done.w_far, ...), custom_call_target="tpu_custom_call" | custom-call | flops 939524096 | bytes 1835008 | tf_op jit(solution)/shard_map/pallas_call | solution.py:157
  81.6 0.7 collective-permute-start.11
  82.3 2.6 %collective-permute-start.12 = (bf16[912,256]{1,0:T(8,128)(2,1)S(1)}, bf16[912,256]{1,0:T(8,128)(2,1)S(1)}, u32[]{:S(2)}, u32[]{:S(2)}) collective-permute-start(bf16[912,256]{1,0:T(8,128)(2,1)S(1)} %get-tuple-element.23), channel_id=1, source_target_pairs={{0,112},{16,0},{32,16},{48,32},{64,48},{80,64},{96,80},{112,96},{1... | collective-permute-start | bytes 1400840 | tf_op jit(solution)/shard_map/ppermute | solution.py:273
  84.9 4.8 %shard_map.79 = (bf16[912,256]{1,0:T(8,128)(2,1)S(1)}, bf16[912,256]{1,0:T(8,128)(2,1)}) custom-call(bf16[4,3,32,1024]{3,2,1,0:T(8,128)(2,1)} %pad_maximum_fusion.1.mine, bf16[4,3,32,1024]{3,2,1,0:T(8,128)(2,1)} %collective-permute-done.8.other, bf16[1792,512]{1,0:T(8,128)(2,1)S(1)} %copy-done.1, bf16[1792,512]{1,0:T(8,128)(2,1)} %collective-permute-done.w_far, ...), custom_call_target="tpu_custom_call" | custom-call | flops 939524096 | bytes 1835008 | tf_op jit(solution)/shard_map/pallas_call | solution.py:157
  89.7 0.1 collective-permute-start.10
  89.8 2.0 %collective-permute-start.9 = (bf16[912,256]{1,0:T(8,128)(2,1)S(1)}, bf16[912,256]{1,0:T(8,128)(2,1)}, u32[]{:S(2)}, u32[]{:S(2)}) collective-permute-start(bf16[912,256]{1,0:T(8,128)(2,1)S(1)} %get-tuple-element.21.refs_2_), channel_id=1, source_target_pairs={{0,16},{16,32},{32,48},{48,64},{64,80},{80,96},{96,112},{112,0},{1... | collective-permute-start | bytes 1400840 | tf_op jit(solution)/shard_map/ppermute | solution.py:273
  91.8 4.7 %collective-permute-done.11.refs_0_ = bf16[912,256]{1,0:T(8,128)(2,1)S(1)} collective-permute-done((bf16[912,256]{1,0:T(8,128)(2,1)S(1)}, bf16[912,256]{1,0:T(8,128)(2,1)S(1)}, u32[]{:S(2)}, u32[]{:S(2)}) %collective-permute-start.11) | collective-permute-done | bytes 466976 | tf_op jit(solution)/shard_map/ppermute | solution.py:273
  96.5 5.2 %shard_map.80 = (bf16[912,256]{1,0:T(8,128)(2,1)}, bf16[912,256]{1,0:T(8,128)(2,1)}) custom-call(bf16[4,3,32,1024]{3,2,1,0:T(8,128)(2,1)} %pad_maximum_fusion.1.mine, bf16[4,3,32,1024]{3,2,1,0:T(8,128)(2,1)} %collective-permute-done.8.other, bf16[1792,512]{1,0:T(8,128)(2,1)S(1)} %copy-done.1, bf16[1792,512]{1,0:T(8,128)(2,1)} %collective-permute-done.w_far, ...), custom_call_target="tpu_custom_call" | custom-call | flops 939524096 | bytes 1835008 | tf_op jit(solution)/shard_map/pallas_call | solution.py:157
  101.7 0.1 collective-permute-start.15
  101.8 3.3 %collective-permute-start.16 = (bf16[912,256]{1,0:T(8,128)(2,1)}, bf16[912,256]{1,0:T(8,128)(2,1)}, u32[]{:S(2)}, u32[]{:S(2)}) collective-permute-start(bf16[912,256]{1,0:T(8,128)(2,1)} %get-tuple-element.27), channel_id=1, source_target_pairs={{0,112},{16,0},{32,16},{48,32},{64,48},{80,64},{96,80},{112,96},{1... | collective-permute-start | bytes 1400840 | tf_op jit(solution)/shard_map/ppermute | solution.py:273
  105.1 1.4 collective-permute-start.23
  106.5 0.1 collective-permute-done.9.refs_0_
  106.6 5.3 %shard_map.81 = (bf16[912,256]{1,0:T(8,128)(2,1)}, bf16[912,256]{1,0:T(8,128)(2,1)}) custom-call(bf16[4,4,32,1024]{3,2,1,0:T(8,128)(2,1)} %pad_maximum_fusion.mine, bf16[4,4,32,1024]{3,2,1,0:T(8,128)(2,1)} %collective-permute-done.4.other, bf16[1792,512]{1,0:T(8,128)(2,1)S(1)} %copy-done.1, bf16[1792,512]{1,0:T(8,128)(2,1)} %collective-permute-done.w_far, ...), custom_call_target="tpu_custom_call" | custom-call | flops 939524096 | bytes 1835008 | tf_op jit(solution)/shard_map/pallas_call | solution.py:157
  111.9 0.1 collective-permute-start.13
  112.0 3.5 %collective-permute-start.14 = (bf16[912,256]{1,0:T(8,128)(2,1)}, bf16[912,256]{1,0:T(8,128)(2,1)}, u32[]{:S(2)}, u32[]{:S(2)}) collective-permute-start(bf16[912,256]{1,0:T(8,128)(2,1)} %get-tuple-element.26), channel_id=1, source_target_pairs={{0,112},{16,0},{32,16},{48,32},{64,48},{80,64},{96,80},{112,96},{1... | collective-permute-start | bytes 1400840 | tf_op jit(solution)/shard_map/ppermute | solution.py:273
  115.5 1.4 collective-permute-done.15.refs_0_
  117.0 5.3 %shard_map.82 = (bf16[912,256]{1,0:T(8,128)(2,1)}, bf16[912,256]{1,0:T(8,128)(2,1)}) custom-call(bf16[4,4,32,1024]{3,2,1,0:T(8,128)(2,1)} %pad_maximum_fusion.mine, bf16[4,4,32,1024]{3,2,1,0:T(8,128)(2,1)} %collective-permute-done.4.other, bf16[1792,512]{1,0:T(8,128)(2,1)S(1)} %copy-done.1, bf16[1792,512]{1,0:T(8,128)(2,1)} %collective-permute-done.w_far, ...), custom_call_target="tpu_custom_call" | custom-call | flops 939524096 | bytes 1835008 | tf_op jit(solution)/shard_map/pallas_call | solution.py:157
  122.3 0.1 collective-permute-start.19
  122.3 3.2 %collective-permute-start.20 = (bf16[912,256]{1,0:T(8,128)(2,1)}, bf16[912,256]{1,0:T(8,128)(2,1)}, u32[]{:S(2)}, u32[]{:S(2)}) collective-permute-start(bf16[912,256]{1,0:T(8,128)(2,1)} %get-tuple-element.31), channel_id=1, source_target_pairs={{0,112},{16,0},{32,16},{48,32},{64,48},{80,64},{96,80},{112,96},{1... | collective-permute-start | bytes 1400840 | tf_op jit(solution)/shard_map/ppermute | solution.py:273
  125.6 0.8 broadcast_in_dim.5
  126.4 4.8 %all-to-all-start.3 = ((f32[16,32,256]{2,1,0:T(8,128)}), f32[16,32,256]{2,1,0:T(8,128)}, u32[]{:S(2)}, u32[]{:S(2)}) async-start(f32[16,32,256]{2,1,0:T(8,128)} %broadcast_in_dim.5), calls=%async_computation.3 | async-start | bytes 1048576 | tf_op jit(solution)/shard_map/all_to_all | solution.py:259
  131.3 1.1 constant_dynamic-slice_fusion.4
  132.4 5.3 %shard_map.83 = (bf16[912,256]{1,0:T(8,128)(2,1)}, bf16[912,256]{1,0:T(8,128)(2,1)}) custom-call(bf16[4,4,32,1024]{3,2,1,0:T(8,128)(2,1)} %pad_maximum_fusion.mine, bf16[4,4,32,1024]{3,2,1,0:T(8,128)(2,1)} %collective-permute-done.4.other, bf16[1792,512]{1,0:T(8,128)(2,1)S(1)} %copy-done.1, bf16[1792,512]{1,0:T(8,128)(2,1)} %collective-permute-done.w_far, ...), custom_call_target="tpu_custom_call" | custom-call | flops 939524096 | bytes 1835008 | tf_op jit(solution)/shard_map/pallas_call | solution.py:157
  137.7 0.1 collective-permute-start.17
  137.8 3.2 %collective-permute-start.18 = (bf16[912,256]{1,0:T(8,128)(2,1)}, bf16[912,256]{1,0:T(8,128)(2,1)}, u32[]{:S(2)}, u32[]{:S(2)}) collective-permute-start(bf16[912,256]{1,0:T(8,128)(2,1)} %get-tuple-element.30), channel_id=1, source_target_pairs={{0,112},{16,0},{32,16},{48,32},{64,48},{80,64},{96,80},{112,96},{1... | collective-permute-start | bytes 1400840 | tf_op jit(solution)/shard_map/ppermute | solution.py:273
  141.0 5.2 %shard_map.85 = (bf16[912,256]{1,0:T(8,128)(2,1)}, bf16[912,256]{1,0:T(8,128)(2,1)}) custom-call(bf16[4,4,32,1024]{3,2,1,0:T(8,128)(2,1)} %pad_maximum_fusion.mine, bf16[4,4,32,1024]{3,2,1,0:T(8,128)(2,1)} %collective-permute-done.4.other, bf16[1792,512]{1,0:T(8,128)(2,1)S(1)} %copy-done.1, bf16[1792,512]{1,0:T(8,128)(2,1)} %collective-permute-done.w_far, ...), custom_call_target="tpu_custom_call" | custom-call | flops 939524096 | bytes 1835008 | tf_op jit(solution)/shard_map/pallas_call | solution.py:157
  146.2 0.1 collective-permute-start.21
  146.3 3.2 %collective-permute-start.22 = (bf16[912,256]{1,0:T(8,128)(2,1)}, bf16[912,256]{1,0:T(8,128)(2,1)}, u32[]{:S(2)}, u32[]{:S(2)}) collective-permute-start(bf16[912,256]{1,0:T(8,128)(2,1)} %get-tuple-element.33), channel_id=1, source_target_pairs={{0,112},{16,0},{32,16},{48,32},{64,48},{80,64},{96,80},{112,96},{1... | collective-permute-start | bytes 1400840 | tf_op jit(solution)/shard_map/ppermute | solution.py:273
  149.6 1.1 copy.15
  150.7 1.1 convolution_multiply_fusion
  151.8 0.9 collective-permute-done.17.right
  152.8 3.2 %shard_map.84.before = f32[1792,256]{1,0:T(8,128)S(1)} custom-call(s32[2]{0:T(128)S(1)} %pad_add_fusion.place, bf16[256,1024]{1,0:T(8,128)(2,1)S(1)} %pad_maximum_fusion.2.own, bf16[1792,512]{1,0:T(8,128)(2,1)S(1)} %copy-done.1, bf16[1792,512]{1,0:T(8,128)(2,1)} %collective-permute-done.w_far, bf16[912,256]{1,0:T(8,128)(2,1)} %collective-permute-done.17.right, ...), custom_call_target="tpu_custom_call" | custom-call | flops 939524096 | bytes 1835008 | tf_op jit(solution)/shard_map/pallas_call | solution.py:188
  156.0 6.0 %collective-permute-done.21.right = bf16[912,256]{1,0:T(8,128)(2,1)} collective-permute-done((bf16[912,256]{1,0:T(8,128)(2,1)}, bf16[912,256]{1,0:T(8,128)(2,1)}, u32[]{:S(2)}, u32[]{:S(2)}) %collective-permute-start.21) | collective-permute-done | bytes 466976 | tf_op jit(solution)/shard_map/ppermute | solution.py:273
  162.0 2.9 %shard_map.86 = bf16[256,1792]{1,0:T(8,128)(2,1)} custom-call(s32[2]{0:T(128)S(1)} %pad_add_fusion.place, f32[1792,256]{1,0:T(8,128)S(1)} %shard_map.84.before, bf16[912,256]{1,0:T(8,128)(2,1)} %collective-permute-done.21.right, bf16[912,256]{1,0:T(8,128)(2,1)} %collective-permute-done.22.left), custom_call_target="tpu_custom_call" | custom-call | tf_op jit(solution)/shard_map/pallas_call | solution.py:196
  (32 shorter events, 0.4 us)
Async XLA Ops:
  0.6 14.2 %copy-start = (bf16[8192,64]{0,1:T(8,128)(2,1)S(1)}, bf16[8192,64]{0,1:T(8,128)(2,1)}, u32[]{:S(2)}) copy-start(bf16[8192,64]{0,1:T(8,128)(2,1)} %param.10) | copy-start | bytes 3145732
  0.6 11.0 %copy-start.1 = (bf16[1792,512]{1,0:T(8,128)(2,1)S(1)}, bf16[1792,512]{1,0:T(8,128)(2,1)}, u32[]{:S(2)}) copy-start(bf16[1792,512]{1,0:T(8,128)(2,1)} %w_down.15) | copy-start | bytes 5505028
  3.2 26.0 %all-to-all-start = ((bf16[8,32,1024]{2,1,0:T(8,128)(2,1)}), bf16[8,32,1024]{2,1,0:T(8,128)(2,1)S(1)}, u32[]{:S(2)}, u32[]{:S(2)}) async-start(bf16[8,32,1024]{2,1,0:T(8,128)(2,1)} %maximum_bitcast_fusion), calls=%async_computation | async-start | bytes 1048576 | tf_op jit(solution)/shard_map/all_to_all | solution.py:230
  11.7 66.0 %collective-permute-start = (bf16[1792,512]{1,0:T(8,128)(2,1)S(1)}, bf16[1792,512]{1,0:T(8,128)(2,1)}, u32[]{:S(2)}, u32[]{:S(2)}) collective-permute-start(bf16[1792,512]{1,0:T(8,128)(2,1)S(1)} %copy-done.1), channel_id=1, source_target_pairs={{0,128},{16,144},{32,160},{48,176},{64,192},{80,208},{96,224},{112... | collective-permute-start | bytes 5505032 | tf_op jit(solution)/shard_map/ppermute | solution.py:217
  29.1 0.8 copy-start.2
  31.8 11.9 %collective-permute-start.5 = (bf16[3,32,1024]{2,1,0:T(8,128)(2,1)}, bf16[3,32,1024]{2,1,0:T(8,128)(2,1)S(1)}, u32[]{:S(2)}, u32[]{:S(2)}) collective-permute-start(bf16[3,32,1024]{2,1,0:T(8,128)(2,1)} %get-tuple-element.19), channel_id=1, source_target_pairs={{0,6},{1,7},{2,0},{3,1},{4,2},{5,3},{6,4},{7,5},{8,14},{9,15},{10,... | collective-permute-start | bytes 589832 | tf_op jit(solution)/shard_map/ppermute | solution.py:248
  34.8 9.6 %collective-permute-start.6 = (bf16[3,32,1024]{2,1,0:T(8,128)(2,1)}, bf16[3,32,1024]{2,1,0:T(8,128)(2,1)S(1)}, u32[]{:S(2)}, u32[]{:S(2)}) collective-permute-start(bf16[3,32,1024]{2,1,0:T(8,128)(2,1)} %get-tuple-element.19), channel_id=1, source_target_pairs={{0,4},{1,5},{2,6},{3,7},{4,0},{5,1},{6,2},{7,3},{8,12},{9,13},{10,... | collective-permute-start | bytes 589832 | tf_op jit(solution)/shard_map/ppermute | solution.py:248
  35.4 11.8 %collective-permute-start.7 = (bf16[3,32,1024]{2,1,0:T(8,128)(2,1)}, bf16[3,32,1024]{2,1,0:T(8,128)(2,1)S(1)}, u32[]{:S(2)}, u32[]{:S(2)}) collective-permute-start(bf16[3,32,1024]{2,1,0:T(8,128)(2,1)} %get-tuple-element.19), channel_id=1, source_target_pairs={{0,2},{1,3},{2,4},{3,5},{4,6},{5,7},{6,0},{7,1},{8,10},{9,11},{10,... | collective-permute-start | bytes 589832 | tf_op jit(solution)/shard_map/ppermute | solution.py:248
  49.2 28.4 %collective-permute-start.8 = (bf16[4,3,32,1024]{3,2,1,0:T(8,128)(2,1)}, bf16[4,3,32,1024]{3,2,1,0:T(8,128)(2,1)}, u32[]{:S(2)}, u32[]{:S(2)}) collective-permute-start(bf16[4,3,32,1024]{3,2,1,0:T(8,128)(2,1)} %pad_maximum_fusion.1.mine), channel_id=1, source_target_pairs={{0,1},{1,0},{2,3},{3,2},{4,5},{5,4},{6,7},{7,6},{8,9},{9,8},{10,11... | collective-permute-start | bytes 2359304 | tf_op jit(solution)/shard_map/ppermute | solution.py:249
  49.3 20.6 %collective-permute-start.1 = (bf16[4,32,1024]{2,1,0:T(8,128)(2,1)}, bf16[4,32,1024]{2,1,0:T(8,128)(2,1)S(1)}, u32[]{:S(2)}, u32[]{:S(2)}) collective-permute-start(bf16[4,32,1024]{2,1,0:T(8,128)(2,1)} %get-tuple-element.18), channel_id=1, source_target_pairs={{0,6},{1,7},{2,0},{3,1},{4,2},{5,3},{6,4},{7,5},{8,14},{9,15},{10,... | collective-permute-start | bytes 786440 | tf_op jit(solution)/shard_map/ppermute | solution.py:248
  49.8 20.1 %collective-permute-start.2 = (bf16[4,32,1024]{2,1,0:T(8,128)(2,1)}, bf16[4,32,1024]{2,1,0:T(8,128)(2,1)S(1)}, u32[]{:S(2)}, u32[]{:S(2)}) collective-permute-start(bf16[4,32,1024]{2,1,0:T(8,128)(2,1)} %get-tuple-element.18), channel_id=1, source_target_pairs={{0,4},{1,5},{2,6},{3,7},{4,0},{5,1},{6,2},{7,3},{8,12},{9,13},{10,... | collective-permute-start | bytes 786440 | tf_op jit(solution)/shard_map/ppermute | solution.py:248
  50.4 19.5 %collective-permute-start.3 = (bf16[4,32,1024]{2,1,0:T(8,128)(2,1)}, bf16[4,32,1024]{2,1,0:T(8,128)(2,1)}, u32[]{:S(2)}, u32[]{:S(2)}) collective-permute-start(bf16[4,32,1024]{2,1,0:T(8,128)(2,1)} %get-tuple-element.18), channel_id=1, source_target_pairs={{0,2},{1,3},{2,4},{3,5},{4,6},{5,7},{6,0},{7,1},{8,10},{9,11},{10,... | collective-permute-start | bytes 786440 | tf_op jit(solution)/shard_map/ppermute | solution.py:248
  66.6 11.0 %all-to-all-start.2 = ((f32[8,2,256]{2,1,0:T(2,128)}), f32[8,2,256]{2,1,0:T(2,128)S(1)}, u32[]{:S(2)}, u32[]{:S(2)}) async-start(f32[8,2,256]{2,1,0:T(2,128)} %broadcast_in_dim.4), calls=%async_computation.2 | async-start | bytes 32768 | tf_op jit(solution)/shard_map/all_to_all | solution.py:253
  72.1 33.0 %collective-permute-start.4 = (bf16[4,4,32,1024]{3,2,1,0:T(8,128)(2,1)}, bf16[4,4,32,1024]{3,2,1,0:T(8,128)(2,1)}, u32[]{:S(2)}, u32[]{:S(2)}) collective-permute-start(bf16[4,4,32,1024]{3,2,1,0:T(8,128)(2,1)} %pad_maximum_fusion.mine), channel_id=1, source_target_pairs={{0,1},{1,0},{2,3},{3,2},{4,5},{5,4},{6,7},{7,6},{8,9},{9,8},{10,11... | collective-permute-start | bytes 3145736 | tf_op jit(solution)/shard_map/ppermute | solution.py:249
  81.6 14.9 %collective-permute-start.11 = (bf16[912,256]{1,0:T(8,128)(2,1)S(1)}, bf16[912,256]{1,0:T(8,128)(2,1)S(1)}, u32[]{:S(2)}, u32[]{:S(2)}) collective-permute-start(bf16[912,256]{1,0:T(8,128)(2,1)S(1)} %get-tuple-element.20.refs_0_), channel_id=1, source_target_pairs={{0,16},{16,32},{32,48},{48,64},{64,80},{80,96},{96,112},{112,0},{1... | collective-permute-start | bytes 1400840 | tf_op jit(solution)/shard_map/ppermute | solution.py:273
  82.3 14.2 %collective-permute-start.12 = (bf16[912,256]{1,0:T(8,128)(2,1)S(1)}, bf16[912,256]{1,0:T(8,128)(2,1)S(1)}, u32[]{:S(2)}, u32[]{:S(2)}) collective-permute-start(bf16[912,256]{1,0:T(8,128)(2,1)S(1)} %get-tuple-element.23), channel_id=1, source_target_pairs={{0,112},{16,0},{32,16},{48,32},{64,48},{80,64},{96,80},{112,96},{1... | collective-permute-start | bytes 1400840 | tf_op jit(solution)/shard_map/ppermute | solution.py:273
  89.7 16.9 %collective-permute-start.10 = (bf16[912,256]{1,0:T(8,128)(2,1)}, bf16[912,256]{1,0:T(8,128)(2,1)}, u32[]{:S(2)}, u32[]{:S(2)}) collective-permute-start(bf16[912,256]{1,0:T(8,128)(2,1)} %get-tuple-element.22), channel_id=1, source_target_pairs={{0,112},{16,0},{32,16},{48,32},{64,48},{80,64},{96,80},{112,96},{1... | collective-permute-start | bytes 1400840 | tf_op jit(solution)/shard_map/ppermute | solution.py:273
  89.8 16.9 %collective-permute-start.9 = (bf16[912,256]{1,0:T(8,128)(2,1)S(1)}, bf16[912,256]{1,0:T(8,128)(2,1)}, u32[]{:S(2)}, u32[]{:S(2)}) collective-permute-start(bf16[912,256]{1,0:T(8,128)(2,1)S(1)} %get-tuple-element.21.refs_2_), channel_id=1, source_target_pairs={{0,16},{16,32},{32,48},{48,64},{64,80},{80,96},{96,112},{112,0},{1... | collective-permute-start | bytes 1400840 | tf_op jit(solution)/shard_map/ppermute | solution.py:273
  101.7 15.2 %collective-permute-start.15 = (bf16[912,256]{1,0:T(8,128)(2,1)}, bf16[912,256]{1,0:T(8,128)(2,1)}, u32[]{:S(2)}, u32[]{:S(2)}) collective-permute-start(bf16[912,256]{1,0:T(8,128)(2,1)} %get-tuple-element.24.refs_2_), channel_id=1, source_target_pairs={{0,16},{16,32},{32,48},{48,64},{64,80},{80,96},{96,112},{112,0},{1... | collective-permute-start | bytes 1400840 | tf_op jit(solution)/shard_map/ppermute | solution.py:273
  101.8 15.1 %collective-permute-start.16 = (bf16[912,256]{1,0:T(8,128)(2,1)}, bf16[912,256]{1,0:T(8,128)(2,1)}, u32[]{:S(2)}, u32[]{:S(2)}) collective-permute-start(bf16[912,256]{1,0:T(8,128)(2,1)} %get-tuple-element.27), channel_id=1, source_target_pairs={{0,112},{16,0},{32,16},{48,32},{64,48},{80,64},{96,80},{112,96},{1... | collective-permute-start | bytes 1400840 | tf_op jit(solution)/shard_map/ppermute | solution.py:273
  105.1 20.5 %collective-permute-start.23 = (f32[16,256]{1,0:T(8,128)S(1)}, f32[16,256]{1,0:T(8,128)S(1)}, u32[]{:S(2)}, u32[]{:S(2)}) collective-permute-start(f32[16,256]{1,0:T(8,128)S(1)} %reshape.38.refs_0_), channel_id=1, source_target_pairs={{0,128},{16,144},{32,160},{48,176},{64,192},{80,208},{96,224},{112... | collective-permute-start | bytes 49160 | tf_op jit(solution)/shard_map/ppermute | solution.py:256
  111.9 20.5 %collective-permute-start.13 = (bf16[912,256]{1,0:T(8,128)(2,1)}, bf16[912,256]{1,0:T(8,128)(2,1)}, u32[]{:S(2)}, u32[]{:S(2)}) collective-permute-start(bf16[912,256]{1,0:T(8,128)(2,1)} %get-tuple-element.25.refs_2_), channel_id=1, source_target_pairs={{0,16},{16,32},{32,48},{48,64},{64,80},{80,96},{96,112},{112,0},{1... | collective-permute-start | bytes 1400840 | tf_op jit(solution)/shard_map/ppermute | solution.py:273
  112.0 20.4 %collective-permute-start.14 = (bf16[912,256]{1,0:T(8,128)(2,1)}, bf16[912,256]{1,0:T(8,128)(2,1)}, u32[]{:S(2)}, u32[]{:S(2)}) collective-permute-start(bf16[912,256]{1,0:T(8,128)(2,1)} %get-tuple-element.26), channel_id=1, source_target_pairs={{0,112},{16,0},{32,16},{48,32},{64,48},{80,64},{96,80},{112,96},{1... | collective-permute-start | bytes 1400840 | tf_op jit(solution)/shard_map/ppermute | solution.py:273
  122.3 18.7 %collective-permute-start.19 = (bf16[912,256]{1,0:T(8,128)(2,1)}, bf16[912,256]{1,0:T(8,128)(2,1)S(1)}, u32[]{:S(2)}, u32[]{:S(2)}) collective-permute-start(bf16[912,256]{1,0:T(8,128)(2,1)} %get-tuple-element.28.refs_2_), channel_id=1, source_target_pairs={{0,16},{16,32},{32,48},{48,64},{64,80},{80,96},{96,112},{112,0},{1... | collective-permute-start | bytes 1400840 | tf_op jit(solution)/shard_map/ppermute | solution.py:273
  122.3 18.6 %collective-permute-start.20 = (bf16[912,256]{1,0:T(8,128)(2,1)}, bf16[912,256]{1,0:T(8,128)(2,1)}, u32[]{:S(2)}, u32[]{:S(2)}) collective-permute-start(bf16[912,256]{1,0:T(8,128)(2,1)} %get-tuple-element.31), channel_id=1, source_target_pairs={{0,112},{16,0},{32,16},{48,32},{64,48},{80,64},{96,80},{112,96},{1... | collective-permute-start | bytes 1400840 | tf_op jit(solution)/shard_map/ppermute | solution.py:273
  126.4 23.2 %all-to-all-start.3 = ((f32[16,32,256]{2,1,0:T(8,128)}), f32[16,32,256]{2,1,0:T(8,128)}, u32[]{:S(2)}, u32[]{:S(2)}) async-start(f32[16,32,256]{2,1,0:T(8,128)} %broadcast_in_dim.5), calls=%async_computation.3 | async-start | bytes 1048576 | tf_op jit(solution)/shard_map/all_to_all | solution.py:259
  137.7 15.1 %collective-permute-start.17 = (bf16[912,256]{1,0:T(8,128)(2,1)}, bf16[912,256]{1,0:T(8,128)(2,1)}, u32[]{:S(2)}, u32[]{:S(2)}) collective-permute-start(bf16[912,256]{1,0:T(8,128)(2,1)} %get-tuple-element.29.refs_2_), channel_id=1, source_target_pairs={{0,16},{16,32},{32,48},{48,64},{64,80},{80,96},{96,112},{112,0},{1... | collective-permute-start | bytes 1400840 | tf_op jit(solution)/shard_map/ppermute | solution.py:273
  137.7 13.0 %copy-start.3 = (f32[8,4096]{1,0:T(8,128)S(1)}, f32[8,4096]{1,0:T(8,128)}, u32[]{:S(2)}) copy-start(f32[8,4096]{1,0:T(8,128)} %param.11) | copy-start | bytes 393220
  137.8 15.0 %collective-permute-start.18 = (bf16[912,256]{1,0:T(8,128)(2,1)}, bf16[912,256]{1,0:T(8,128)(2,1)}, u32[]{:S(2)}, u32[]{:S(2)}) collective-permute-start(bf16[912,256]{1,0:T(8,128)(2,1)} %get-tuple-element.30), channel_id=1, source_target_pairs={{0,112},{16,0},{32,16},{48,32},{64,48},{80,64},{96,80},{112,96},{1... | collective-permute-start | bytes 1400840 | tf_op jit(solution)/shard_map/ppermute | solution.py:273
  146.2 15.8 %collective-permute-start.21 = (bf16[912,256]{1,0:T(8,128)(2,1)}, bf16[912,256]{1,0:T(8,128)(2,1)}, u32[]{:S(2)}, u32[]{:S(2)}) collective-permute-start(bf16[912,256]{1,0:T(8,128)(2,1)} %get-tuple-element.32), channel_id=1, source_target_pairs={{0,16},{16,32},{32,48},{48,64},{64,80},{80,96},{96,112},{112,0},{1... | collective-permute-start | bytes 1400840 | tf_op jit(solution)/shard_map/ppermute | solution.py:273
  146.3 15.7 %collective-permute-start.22 = (bf16[912,256]{1,0:T(8,128)(2,1)}, bf16[912,256]{1,0:T(8,128)(2,1)}, u32[]{:S(2)}, u32[]{:S(2)}) collective-permute-start(bf16[912,256]{1,0:T(8,128)(2,1)} %get-tuple-element.33), channel_id=1, source_target_pairs={{0,112},{16,0},{32,16},{48,32},{64,48},{80,64},{96,80},{112,96},{1... | collective-permute-start | bytes 1400840 | tf_op jit(solution)/shard_map/ppermute | solution.py:273

commit v2 on v1

--- a/solution.py
+++ b/solution.py
@@ -78,12 +78,15 @@
         if n_in:
             moves.append((came[side], coming.at[side]))
         started = [pltpu.make_async_copy(src, dst, sems.at[side, k]) for k, (src, dst) in enumerate(moves)]
-        for c in started:
-            c.start()
         copies.append(started)
+    for c in copies[0]:
+        c.start()
     for side, (_, part) in enumerate(sides):
         for c in copies[side]:
             c.wait()
+        if side == 0:
+            for c in copies[1]:
+                c.start()
         act = acts[side].reshape(toks, acts.shape[-1])
         add_own(x, w_down.at[pl.ds(part * chunk, chunk)], far.at[side], act)
         if n_in:

time: 166 us -> 166 us (level)
  transfers between devices with their start and end apart: 27 -> 27, of which waited for: 10 -> 9; matrix products, arithmetic and copies ran while one was open for 9% -> 9% of each run, Pallas kernels for 24% -> 24%
where the time goes in v2:
time: 166 us; the launch traced here: 165 us
  starting transfers between devices  48.6 us (29%)
  Pallas kernels  43.3 us (26%)
  waiting for transfers between devices  39.2 us (24%)
  blocking collectives  14.5 us (9%)
  local copies, waits for them, and re-layouts  6.72 us (4%)
  matrix products  6.55 us (4%)
  other arithmetic  5.08 us (3%)
    pallas_call x7, Pallas kernels, stage(): pl.pallas_call(functools.partial(stage_kernel, at_r, at_l, part_r, len(ca...  35.3 us
    ppermute x7, starting transfers between devices, per_device(): lax.ppermute(left, 'dp', Z_PERM[-1])  19 us
    all_to_all x1, blocking collectives, per_device(): summed = lax.all_to_all(part, 'tensor', 0, 0, tiled=True).sum(axis=0)  14.5 us
    ppermute x7, waiting for transfers between devices, per_device(): lax.ppermute(right, 'dp', Z_PERM[1])  13.1 us
    ppermute x6, waiting for transfers between devices, per_device(): lax.ppermute(got, 'tensor', Y_PERM[Y - r])  10.9 us
    all_to_all x1, waiting for transfers between devices, per_device(): lax.all_to_all(columns(own_rows), 'dp', 0, 0, axis_index_groups=rings, ti...  9.82 us
    all_to_all x1, starting transfers between devices, per_device(): lax.all_to_all(columns(own_rows), 'dp', 0, 0, axis_index_groups=rings, ti...  8.47 us
    ppermute x6, starting transfers between devices, per_device(): lax.ppermute(got, 'tensor', Y_PERM[Y - r])  6.69 us
  transfers between devices with their start and end apart: 27, of which 9 were waited for; matrix products, arithmetic and copies ran while one was open for 9% of the time, Pallas kernels for 24%

profile of v2, /device:TPU:6, one launch (start us, length us, event | category | flops | bytes accessed | tf_op | source)
XLA Modules:
  0.0 165.0 jit_solution(13085709849067111145)
XLA Ops:
  0.7 1.2 constant_dynamic-slice_fusion.2
  1.9 0.2 copy.16
  2.2 0.2 copy_bitcast_fusion
  2.3 0.9 maximum_bitcast_fusion
  3.2 8.5 %all-to-all-start = ((bf16[8,32,1024]{2,1,0:T(8,128)(2,1)}), bf16[8,32,1024]{2,1,0:T(8,128)(2,1)S(1)}, u32[]{:S(2)}, u32[]{:S(2)}) async-start(bf16[8,32,1024]{2,1,0:T(8,128)(2,1)} %maximum_bitcast_fusion), calls=%async_computation | async-start | bytes 1048576 | tf_op jit(solution)/shard_map/all_to_all | solution.py:233
  11.7 1.5 collective-permute-start
  13.1 1.6 fusion.2
  14.8 3.6 %fusion = f32[2,128,64]{1,2,0:T(8,128)S(1)} fusion(bf16[2,128,8192]{2,1,0:T(8,128)(2,1)} %param.7, bf16[8192,64]{0,1:T(8,128)(2,1)S(1)} %copy-done), kind=kOutput, calls=%fused_computation.2 | convolution fusion | flops 268435456 | bytes 5308416 | tf_op jit(solution)/shard_map/dot_general | solution.py:236
  18.4 0.2 fusion.4
  18.6 0.1 reshape.37
  18.7 0.6 copy.20
  19.3 9.8 %all-to-all-done.planes = bf16[8,32,1024]{2,1,0:T(8,128)(2,1)S(1)} async-done(((bf16[8,32,1024]{2,1,0:T(8,128)(2,1)}), bf16[8,32,1024]{2,1,0:T(8,128)(2,1)S(1)}, u32[]{:S(2)}, u32[]{:S(2)}) %all-to-all-start) | async-done | bytes 524320 | tf_op jit(solution)/shard_map/all_to_all | solution.py:233
  29.1 0.8 copy-done.2
  29.9 1.9 %shard_map.77 = (bf16[3,32,1024]{2,1,0:T(8,128)(2,1)}, bf16[4,32,1024]{2,1,0:T(8,128)(2,1)}) custom-call(s32[1]{0:T(128)} %bitcast.3.z, bf16[8,32,1024]{2,1,0:T(8,128)(2,1)} %copy-done.2, f32[16,2,256]{2,1,0:T(2,128)} %bitcast.46), custom_call_target="tpu_custom_call" | custom-call | tf_op jit(solution)/shard_map/pallas_call | solution.py:138
  31.8 3.0 %collective-permute-start.5 = (bf16[3,32,1024]{2,1,0:T(8,128)(2,1)}, bf16[3,32,1024]{2,1,0:T(8,128)(2,1)S(1)}, u32[]{:S(2)}, u32[]{:S(2)}) collective-permute-start(bf16[3,32,1024]{2,1,0:T(8,128)(2,1)} %get-tuple-element.19), channel_id=1, source_target_pairs={{0,6},{1,7},{2,0},{3,1},{4,2},{5,3},{6,4},{7,5},{8,14},{9,15},{10,... | collective-permute-start | bytes 589832 | tf_op jit(solution)/shard_map/ppermute | solution.py:251
  34.8 0.6 collective-permute-start.6
  35.4 1.0 collective-permute-start.7
  36.4 7.3 %collective-permute-done.5 = bf16[3,32,1024]{2,1,0:T(8,128)(2,1)S(1)} collective-permute-done((bf16[3,32,1024]{2,1,0:T(8,128)(2,1)}, bf16[3,32,1024]{2,1,0:T(8,128)(2,1)S(1)}, u32[]{:S(2)}, u32[]{:S(2)}) %collective-permute-start.5) | collective-permute-done | bytes 196640 | tf_op jit(solution)/shard_map/ppermute | solution.py:251
  43.7 0.7 collective-permute-done.6
  44.4 2.9 %collective-permute-done.7 = bf16[3,32,1024]{2,1,0:T(8,128)(2,1)S(1)} collective-permute-done((bf16[3,32,1024]{2,1,0:T(8,128)(2,1)}, bf16[3,32,1024]{2,1,0:T(8,128)(2,1)S(1)}, u32[]{:S(2)}, u32[]{:S(2)}) %collective-permute-start.7) | collective-permute-done | bytes 196640 | tf_op jit(solution)/shard_map/ppermute | solution.py:251
  47.3 1.9 %pad_maximum_fusion.1.mine = bf16[4,3,32,1024]{3,2,1,0:T(8,128)(2,1)} fusion(bf16[1,3,32,1024]{3,2,1,0:T(8,128)(2,1)S(1)} %bitcast.54, bf16[1,3,32,1024]{3,2,1,0:T(8,128)(2,1)S(1)} %bitcast.53, bf16[1,3,32,1024]{3,2,1,0:T(8,128)(2,1)S(1)} %bitcast.52, bf16[1,3,32,1024]{3,2,1,0:T(8,128)(2,1)} %bitcast.51), kind=kLoop, calls=%fused_computation.4 | loop fusion | flops 1179648 | bytes 1572864 | tf_op jit(solution)/shard_map/stack | solution.py:251
  49.2 0.1 collective-permute-start.8
  49.3 0.5 collective-permute-start.1
  49.8 0.6 collective-permute-start.2
  50.4 1.0 collective-permute-start.3
  51.4 14.5 %all_to_all.20 = f32[16,2,256]{2,1,0:T(2,128)S(1)} all-to-all(f32[16,2,256]{2,1,0:T(2,128)} %bitcast.47), channel_id=1, replica_groups=mesh['dp'=16,'tensor'=16] {'tensor'}, dimensions={0} | all-to-all | bytes 65536 | tf_op jit(solution)/shard_map/all_to_all | solution.py:246
  66.0 0.6 broadcast_in_dim.4
  66.6 3.3 %all-to-all-start.2 = ((f32[8,2,256]{2,1,0:T(2,128)}), f32[8,2,256]{2,1,0:T(2,128)S(1)}, u32[]{:S(2)}, u32[]{:S(2)}) async-start(f32[8,2,256]{2,1,0:T(2,128)} %broadcast_in_dim.4), calls=%async_computation.2 | async-start | bytes 32768 | tf_op jit(solution)/shard_map/all_to_all | solution.py:256
  69.9 2.2 %pad_maximum_fusion.mine = bf16[4,4,32,1024]{3,2,1,0:T(8,128)(2,1)} fusion(bf16[1,4,32,1024]{3,2,1,0:T(8,128)(2,1)} %bitcast.13, bf16[1,4,32,1024]{3,2,1,0:T(8,128)(2,1)S(1)} %bitcast.50, bf16[1,4,32,1024]{3,2,1,0:T(8,128)(2,1)S(1)} %bitcast.49, bf16[1,4,32,1024]{3,2,1,0:T(8,128)(2,1)} %bitcast.48), kind=kLoop, calls=%fused_computation.1 | loop fusion | flops 1572864 | bytes 2097152 | tf_op jit(solution)/shard_map/stack | solution.py:251
  72.1 0.1 collective-permute-start.4
  72.2 5.4 %all-to-all-done.2 = f32[8,2,256]{2,1,0:T(2,128)S(1)} async-done(((f32[8,2,256]{2,1,0:T(2,128)}), f32[8,2,256]{2,1,0:T(2,128)S(1)}, u32[]{:S(2)}, u32[]{:S(2)}) %all-to-all-start.2) | async-done | bytes 16416 | tf_op jit(solution)/shard_map/all_to_all | solution.py:256
  77.6 4.0 %shard_map.78 = (bf16[912,256]{1,0:T(8,128)(2,1)S(1)}, bf16[912,256]{1,0:T(8,128)(2,1)S(1)}) custom-call(bf16[4,3,32,1024]{3,2,1,0:T(8,128)(2,1)} %pad_maximum_fusion.1.mine, bf16[4,3,32,1024]{3,2,1,0:T(8,128)(2,1)} %collective-permute-done.8.other, bf16[1792,512]{1,0:T(8,128)(2,1)S(1)} %copy-done.1, bf16[1792,512]{1,0:T(8,128)(2,1)} %collective-permute-done.w_far, ...), custom_call_target="tpu_custom_call" | custom-call | flops 939524096 | bytes 1835008 | tf_op jit(solution)/shard_map/pallas_call | solution.py:160
  81.7 0.7 collective-permute-start.11
  82.4 2.6 %collective-permute-start.12 = (bf16[912,256]{1,0:T(8,128)(2,1)S(1)}, bf16[912,256]{1,0:T(8,128)(2,1)S(1)}, u32[]{:S(2)}, u32[]{:S(2)}) collective-permute-start(bf16[912,256]{1,0:T(8,128)(2,1)S(1)} %get-tuple-element.23), channel_id=1, source_target_pairs={{0,112},{16,0},{32,16},{48,32},{64,48},{80,64},{96,80},{112,96},{1... | collective-permute-start | bytes 1400840 | tf_op jit(solution)/shard_map/ppermute | solution.py:276
  85.0 4.8 %shard_map.79 = (bf16[912,256]{1,0:T(8,128)(2,1)S(1)}, bf16[912,256]{1,0:T(8,128)(2,1)}) custom-call(bf16[4,3,32,1024]{3,2,1,0:T(8,128)(2,1)} %pad_maximum_fusion.1.mine, bf16[4,3,32,1024]{3,2,1,0:T(8,128)(2,1)} %collective-permute-done.8.other, bf16[1792,512]{1,0:T(8,128)(2,1)S(1)} %copy-done.1, bf16[1792,512]{1,0:T(8,128)(2,1)} %collective-permute-done.w_far, ...), custom_call_target="tpu_custom_call" | custom-call | flops 939524096 | bytes 1835008 | tf_op jit(solution)/shard_map/pallas_call | solution.py:160
  89.8 0.1 collective-permute-start.10
  89.9 2.0 %collective-permute-start.9 = (bf16[912,256]{1,0:T(8,128)(2,1)S(1)}, bf16[912,256]{1,0:T(8,128)(2,1)}, u32[]{:S(2)}, u32[]{:S(2)}) collective-permute-start(bf16[912,256]{1,0:T(8,128)(2,1)S(1)} %get-tuple-element.21.refs_2_), channel_id=1, source_target_pairs={{0,16},{16,32},{32,48},{48,64},{64,80},{80,96},{96,112},{112,0},{1... | collective-permute-start | bytes 1400840 | tf_op jit(solution)/shard_map/ppermute | solution.py:276
  91.9 4.7 %collective-permute-done.11.refs_0_ = bf16[912,256]{1,0:T(8,128)(2,1)S(1)} collective-permute-done((bf16[912,256]{1,0:T(8,128)(2,1)S(1)}, bf16[912,256]{1,0:T(8,128)(2,1)S(1)}, u32[]{:S(2)}, u32[]{:S(2)}) %collective-permute-start.11) | collective-permute-done | bytes 466976 | tf_op jit(solution)/shard_map/ppermute | solution.py:276
  96.6 5.5 %shard_map.80 = (bf16[912,256]{1,0:T(8,128)(2,1)}, bf16[912,256]{1,0:T(8,128)(2,1)}) custom-call(bf16[4,3,32,1024]{3,2,1,0:T(8,128)(2,1)} %pad_maximum_fusion.1.mine, bf16[4,3,32,1024]{3,2,1,0:T(8,128)(2,1)} %collective-permute-done.8.other, bf16[1792,512]{1,0:T(8,128)(2,1)S(1)} %copy-done.1, bf16[1792,512]{1,0:T(8,128)(2,1)} %collective-permute-done.w_far, ...), custom_call_target="tpu_custom_call" | custom-call | flops 939524096 | bytes 1835008 | tf_op jit(solution)/shard_map/pallas_call | solution.py:160
  102.1 0.1 collective-permute-start.15
  102.2 3.3 %collective-permute-start.16 = (bf16[912,256]{1,0:T(8,128)(2,1)}, bf16[912,256]{1,0:T(8,128)(2,1)}, u32[]{:S(2)}, u32[]{:S(2)}) collective-permute-start(bf16[912,256]{1,0:T(8,128)(2,1)} %get-tuple-element.27), channel_id=1, source_target_pairs={{0,112},{16,0},{32,16},{48,32},{64,48},{80,64},{96,80},{112,96},{1... | collective-permute-start | bytes 1400840 | tf_op jit(solution)/shard_map/ppermute | solution.py:276
  105.5 1.4 collective-permute-start.23
  106.9 5.3 %shard_map.81 = (bf16[912,256]{1,0:T(8,128)(2,1)}, bf16[912,256]{1,0:T(8,128)(2,1)}) custom-call(bf16[4,4,32,1024]{3,2,1,0:T(8,128)(2,1)} %pad_maximum_fusion.mine, bf16[4,4,32,1024]{3,2,1,0:T(8,128)(2,1)} %collective-permute-done.4.other, bf16[1792,512]{1,0:T(8,128)(2,1)S(1)} %copy-done.1, bf16[1792,512]{1,0:T(8,128)(2,1)} %collective-permute-done.w_far, ...), custom_call_target="tpu_custom_call" | custom-call | flops 939524096 | bytes 1835008 | tf_op jit(solution)/shard_map/pallas_call | solution.py:160
  112.2 0.1 collective-permute-start.13
  112.2 3.4 %collective-permute-start.14 = (bf16[912,256]{1,0:T(8,128)(2,1)}, bf16[912,256]{1,0:T(8,128)(2,1)}, u32[]{:S(2)}, u32[]{:S(2)}) collective-permute-start(bf16[912,256]{1,0:T(8,128)(2,1)} %get-tuple-element.26), channel_id=1, source_target_pairs={{0,112},{16,0},{32,16},{48,32},{64,48},{80,64},{96,80},{112,96},{1... | collective-permute-start | bytes 1400840 | tf_op jit(solution)/shard_map/ppermute | solution.py:276
  115.6 1.5 collective-permute-done.15.refs_0_
  117.1 5.3 %shard_map.82 = (bf16[912,256]{1,0:T(8,128)(2,1)}, bf16[912,256]{1,0:T(8,128)(2,1)}) custom-call(bf16[4,4,32,1024]{3,2,1,0:T(8,128)(2,1)} %pad_maximum_fusion.mine, bf16[4,4,32,1024]{3,2,1,0:T(8,128)(2,1)} %collective-permute-done.4.other, bf16[1792,512]{1,0:T(8,128)(2,1)S(1)} %copy-done.1, bf16[1792,512]{1,0:T(8,128)(2,1)} %collective-permute-done.w_far, ...), custom_call_target="tpu_custom_call" | custom-call | flops 939524096 | bytes 1835008 | tf_op jit(solution)/shard_map/pallas_call | solution.py:160
  122.4 0.1 collective-permute-start.19
  122.5 3.2 %collective-permute-start.20 = (bf16[912,256]{1,0:T(8,128)(2,1)}, bf16[912,256]{1,0:T(8,128)(2,1)}, u32[]{:S(2)}, u32[]{:S(2)}) collective-permute-start(bf16[912,256]{1,0:T(8,128)(2,1)} %get-tuple-element.31), channel_id=1, source_target_pairs={{0,112},{16,0},{32,16},{48,32},{64,48},{80,64},{96,80},{112,96},{1... | collective-permute-start | bytes 1400840 | tf_op jit(solution)/shard_map/ppermute | solution.py:276
  125.7 0.8 broadcast_in_dim.5
  126.6 4.8 %all-to-all-start.3 = ((f32[16,32,256]{2,1,0:T(8,128)}), f32[16,32,256]{2,1,0:T(8,128)}, u32[]{:S(2)}, u32[]{:S(2)}) async-start(f32[16,32,256]{2,1,0:T(8,128)} %broadcast_in_dim.5), calls=%async_computation.3 | async-start | bytes 1048576 | tf_op jit(solution)/shard_map/all_to_all | solution.py:262
  131.4 1.1 constant_dynamic-slice_fusion.4
  132.5 5.3 %shard_map.83 = (bf16[912,256]{1,0:T(8,128)(2,1)}, bf16[912,256]{1,0:T(8,128)(2,1)}) custom-call(bf16[4,4,32,1024]{3,2,1,0:T(8,128)(2,1)} %pad_maximum_fusion.mine, bf16[4,4,32,1024]{3,2,1,0:T(8,128)(2,1)} %collective-permute-done.4.other, bf16[1792,512]{1,0:T(8,128)(2,1)S(1)} %copy-done.1, bf16[1792,512]{1,0:T(8,128)(2,1)} %collective-permute-done.w_far, ...), custom_call_target="tpu_custom_call" | custom-call | flops 939524096 | bytes 1835008 | tf_op jit(solution)/shard_map/pallas_call | solution.py:160
  137.8 0.1 collective-permute-start.17
  137.9 3.2 %collective-permute-start.18 = (bf16[912,256]{1,0:T(8,128)(2,1)}, bf16[912,256]{1,0:T(8,128)(2,1)}, u32[]{:S(2)}, u32[]{:S(2)}) collective-permute-start(bf16[912,256]{1,0:T(8,128)(2,1)} %get-tuple-element.30), channel_id=1, source_target_pairs={{0,112},{16,0},{32,16},{48,32},{64,48},{80,64},{96,80},{112,96},{1... | collective-permute-start | bytes 1400840 | tf_op jit(solution)/shard_map/ppermute | solution.py:276
  141.1 5.2 %shard_map.85 = (bf16[912,256]{1,0:T(8,128)(2,1)}, bf16[912,256]{1,0:T(8,128)(2,1)}) custom-call(bf16[4,4,32,1024]{3,2,1,0:T(8,128)(2,1)} %pad_maximum_fusion.mine, bf16[4,4,32,1024]{3,2,1,0:T(8,128)(2,1)} %collective-permute-done.4.other, bf16[1792,512]{1,0:T(8,128)(2,1)S(1)} %copy-done.1, bf16[1792,512]{1,0:T(8,128)(2,1)} %collective-permute-done.w_far, ...), custom_call_target="tpu_custom_call" | custom-call | flops 939524096 | bytes 1835008 | tf_op jit(solution)/shard_map/pallas_call | solution.py:160
  146.3 0.1 collective-permute-start.21
  146.4 3.2 %collective-permute-start.22 = (bf16[912,256]{1,0:T(8,128)(2,1)}, bf16[912,256]{1,0:T(8,128)(2,1)}, u32[]{:S(2)}, u32[]{:S(2)}) collective-permute-start(bf16[912,256]{1,0:T(8,128)(2,1)} %get-tuple-element.33), channel_id=1, source_target_pairs={{0,112},{16,0},{32,16},{48,32},{64,48},{80,64},{96,80},{112,96},{1... | collective-permute-start | bytes 1400840 | tf_op jit(solution)/shard_map/ppermute | solution.py:276
  149.7 1.1 copy.15
  150.8 1.1 convolution_multiply_fusion
  152.0 1.0 collective-permute-done.17.right
  152.9 3.2 %shard_map.84.before = f32[1792,256]{1,0:T(8,128)S(1)} custom-call(s32[2]{0:T(128)S(1)} %pad_add_fusion.place, bf16[256,1024]{1,0:T(8,128)(2,1)S(1)} %pad_maximum_fusion.2.own, bf16[1792,512]{1,0:T(8,128)(2,1)S(1)} %copy-done.1, bf16[1792,512]{1,0:T(8,128)(2,1)} %collective-permute-done.w_far, bf16[912,256]{1,0:T(8,128)(2,1)} %collective-permute-done.17.right, ...), custom_call_target="tpu_custom_call" | custom-call | flops 939524096 | bytes 1835008 | tf_op jit(solution)/shard_map/pallas_call | solution.py:191
  156.1 6.0 %collective-permute-done.21.right = bf16[912,256]{1,0:T(8,128)(2,1)} collective-permute-done((bf16[912,256]{1,0:T(8,128)(2,1)}, bf16[912,256]{1,0:T(8,128)(2,1)}, u32[]{:S(2)}, u32[]{:S(2)}) %collective-permute-start.21) | collective-permute-done | bytes 466976 | tf_op jit(solution)/shard_map/ppermute | solution.py:276
  162.1 2.9 %shard_map.86 = bf16[256,1792]{1,0:T(8,128)(2,1)} custom-call(s32[2]{0:T(128)S(1)} %pad_add_fusion.place, f32[1792,256]{1,0:T(8,128)S(1)} %shard_map.84.before, bf16[912,256]{1,0:T(8,128)(2,1)} %collective-permute-done.21.right, bf16[912,256]{1,0:T(8,128)(2,1)} %collective-permute-done.22.left), custom_call_target="tpu_custom_call" | custom-call | tf_op jit(solution)/shard_map/pallas_call | solution.py:199
  (32 shorter events, 0.3 us)
Async XLA Ops:
  0.6 14.2 %copy-start = (bf16[8192,64]{0,1:T(8,128)(2,1)S(1)}, bf16[8192,64]{0,1:T(8,128)(2,1)}, u32[]{:S(2)}) copy-start(bf16[8192,64]{0,1:T(8,128)(2,1)} %param.10) | copy-start | bytes 3145732
  0.6 11.0 %copy-start.1 = (bf16[1792,512]{1,0:T(8,128)(2,1)S(1)}, bf16[1792,512]{1,0:T(8,128)(2,1)}, u32[]{:S(2)}) copy-start(bf16[1792,512]{1,0:T(8,128)(2,1)} %w_down.15) | copy-start | bytes 5505028
  3.2 26.0 %all-to-all-start = ((bf16[8,32,1024]{2,1,0:T(8,128)(2,1)}), bf16[8,32,1024]{2,1,0:T(8,128)(2,1)S(1)}, u32[]{:S(2)}, u32[]{:S(2)}) async-start(bf16[8,32,1024]{2,1,0:T(8,128)(2,1)} %maximum_bitcast_fusion), calls=%async_computation | async-start | bytes 1048576 | tf_op jit(solution)/shard_map/all_to_all | solution.py:233
  11.7 66.0 %collective-permute-start = (bf16[1792,512]{1,0:T(8,128)(2,1)S(1)}, bf16[1792,512]{1,0:T(8,128)(2,1)}, u32[]{:S(2)}, u32[]{:S(2)}) collective-permute-start(bf16[1792,512]{1,0:T(8,128)(2,1)S(1)} %copy-done.1), channel_id=1, source_target_pairs={{0,128},{16,144},{32,160},{48,176},{64,192},{80,208},{96,224},{112... | collective-permute-start | bytes 5505032 | tf_op jit(solution)/shard_map/ppermute | solution.py:220
  29.1 0.8 copy-start.2
  31.8 11.9 %collective-permute-start.5 = (bf16[3,32,1024]{2,1,0:T(8,128)(2,1)}, bf16[3,32,1024]{2,1,0:T(8,128)(2,1)S(1)}, u32[]{:S(2)}, u32[]{:S(2)}) collective-permute-start(bf16[3,32,1024]{2,1,0:T(8,128)(2,1)} %get-tuple-element.19), channel_id=1, source_target_pairs={{0,6},{1,7},{2,0},{3,1},{4,2},{5,3},{6,4},{7,5},{8,14},{9,15},{10,... | collective-permute-start | bytes 589832 | tf_op jit(solution)/shard_map/ppermute | solution.py:251
  34.8 9.6 %collective-permute-start.6 = (bf16[3,32,1024]{2,1,0:T(8,128)(2,1)}, bf16[3,32,1024]{2,1,0:T(8,128)(2,1)S(1)}, u32[]{:S(2)}, u32[]{:S(2)}) collective-permute-start(bf16[3,32,1024]{2,1,0:T(8,128)(2,1)} %get-tuple-element.19), channel_id=1, source_target_pairs={{0,4},{1,5},{2,6},{3,7},{4,0},{5,1},{6,2},{7,3},{8,12},{9,13},{10,... | collective-permute-start | bytes 589832 | tf_op jit(solution)/shard_map/ppermute | solution.py:251
  35.4 11.8 %collective-permute-start.7 = (bf16[3,32,1024]{2,1,0:T(8,128)(2,1)}, bf16[3,32,1024]{2,1,0:T(8,128)(2,1)S(1)}, u32[]{:S(2)}, u32[]{:S(2)}) collective-permute-start(bf16[3,32,1024]{2,1,0:T(8,128)(2,1)} %get-tuple-element.19), channel_id=1, source_target_pairs={{0,2},{1,3},{2,4},{3,5},{4,6},{5,7},{6,0},{7,1},{8,10},{9,11},{10,... | collective-permute-start | bytes 589832 | tf_op jit(solution)/shard_map/ppermute | solution.py:251
  49.2 28.4 %collective-permute-start.8 = (bf16[4,3,32,1024]{3,2,1,0:T(8,128)(2,1)}, bf16[4,3,32,1024]{3,2,1,0:T(8,128)(2,1)}, u32[]{:S(2)}, u32[]{:S(2)}) collective-permute-start(bf16[4,3,32,1024]{3,2,1,0:T(8,128)(2,1)} %pad_maximum_fusion.1.mine), channel_id=1, source_target_pairs={{0,1},{1,0},{2,3},{3,2},{4,5},{5,4},{6,7},{7,6},{8,9},{9,8},{10,11... | collective-permute-start | bytes 2359304 | tf_op jit(solution)/shard_map/ppermute | solution.py:252
  49.3 20.6 %collective-permute-start.1 = (bf16[4,32,1024]{2,1,0:T(8,128)(2,1)}, bf16[4,32,1024]{2,1,0:T(8,128)(2,1)S(1)}, u32[]{:S(2)}, u32[]{:S(2)}) collective-permute-start(bf16[4,32,1024]{2,1,0:T(8,128)(2,1)} %get-tuple-element.18), channel_id=1, source_target_pairs={{0,6},{1,7},{2,0},{3,1},{4,2},{5,3},{6,4},{7,5},{8,14},{9,15},{10,... | collective-permute-start | bytes 786440 | tf_op jit(solution)/shard_map/ppermute | solution.py:251
  49.8 20.1 %collective-permute-start.2 = (bf16[4,32,1024]{2,1,0:T(8,128)(2,1)}, bf16[4,32,1024]{2,1,0:T(8,128)(2,1)S(1)}, u32[]{:S(2)}, u32[]{:S(2)}) collective-permute-start(bf16[4,32,1024]{2,1,0:T(8,128)(2,1)} %get-tuple-element.18), channel_id=1, source_target_pairs={{0,4},{1,5},{2,6},{3,7},{4,0},{5,1},{6,2},{7,3},{8,12},{9,13},{10,... | collective-permute-start | bytes 786440 | tf_op jit(solution)/shard_map/ppermute | solution.py:251
  50.4 19.5 %collective-permute-start.3 = (bf16[4,32,1024]{2,1,0:T(8,128)(2,1)}, bf16[4,32,1024]{2,1,0:T(8,128)(2,1)}, u32[]{:S(2)}, u32[]{:S(2)}) collective-permute-start(bf16[4,32,1024]{2,1,0:T(8,128)(2,1)} %get-tuple-element.18), channel_id=1, source_target_pairs={{0,2},{1,3},{2,4},{3,5},{4,6},{5,7},{6,0},{7,1},{8,10},{9,11},{10,... | collective-permute-start | bytes 786440 | tf_op jit(solution)/shard_map/ppermute | solution.py:251
  66.6 11.0 %all-to-all-start.2 = ((f32[8,2,256]{2,1,0:T(2,128)}), f32[8,2,256]{2,1,0:T(2,128)S(1)}, u32[]{:S(2)}, u32[]{:S(2)}) async-start(f32[8,2,256]{2,1,0:T(2,128)} %broadcast_in_dim.4), calls=%async_computation.2 | async-start | bytes 32768 | tf_op jit(solution)/shard_map/all_to_all | solution.py:256
  72.1 33.4 %collective-permute-start.4 = (bf16[4,4,32,1024]{3,2,1,0:T(8,128)(2,1)}, bf16[4,4,32,1024]{3,2,1,0:T(8,128)(2,1)}, u32[]{:S(2)}, u32[]{:S(2)}) collective-permute-start(bf16[4,4,32,1024]{3,2,1,0:T(8,128)(2,1)} %pad_maximum_fusion.mine), channel_id=1, source_target_pairs={{0,1},{1,0},{2,3},{3,2},{4,5},{5,4},{6,7},{7,6},{8,9},{9,8},{10,11... | collective-permute-start | bytes 3145736 | tf_op jit(solution)/shard_map/ppermute | solution.py:252
  81.7 14.9 %collective-permute-start.11 = (bf16[912,256]{1,0:T(8,128)(2,1)S(1)}, bf16[912,256]{1,0:T(8,128)(2,1)S(1)}, u32[]{:S(2)}, u32[]{:S(2)}) collective-permute-start(bf16[912,256]{1,0:T(8,128)(2,1)S(1)} %get-tuple-element.20.refs_0_), channel_id=1, source_target_pairs={{0,16},{16,32},{32,48},{48,64},{64,80},{80,96},{96,112},{112,0},{1... | collective-permute-start | bytes 1400840 | tf_op jit(solution)/shard_map/ppermute | solution.py:276
  82.4 14.2 %collective-permute-start.12 = (bf16[912,256]{1,0:T(8,128)(2,1)S(1)}, bf16[912,256]{1,0:T(8,128)(2,1)S(1)}, u32[]{:S(2)}, u32[]{:S(2)}) collective-permute-start(bf16[912,256]{1,0:T(8,128)(2,1)S(1)} %get-tuple-element.23), channel_id=1, source_target_pairs={{0,112},{16,0},{32,16},{48,32},{64,48},{80,64},{96,80},{112,96},{1... | collective-permute-start | bytes 1400840 | tf_op jit(solution)/shard_map/ppermute | solution.py:276
  89.8 17.1 %collective-permute-start.10 = (bf16[912,256]{1,0:T(8,128)(2,1)}, bf16[912,256]{1,0:T(8,128)(2,1)}, u32[]{:S(2)}, u32[]{:S(2)}) collective-permute-start(bf16[912,256]{1,0:T(8,128)(2,1)} %get-tuple-element.22), channel_id=1, source_target_pairs={{0,112},{16,0},{32,16},{48,32},{64,48},{80,64},{96,80},{112,96},{1... | collective-permute-start | bytes 1400840 | tf_op jit(solution)/shard_map/ppermute | solution.py:276
  89.9 17.0 %collective-permute-start.9 = (bf16[912,256]{1,0:T(8,128)(2,1)S(1)}, bf16[912,256]{1,0:T(8,128)(2,1)}, u32[]{:S(2)}, u32[]{:S(2)}) collective-permute-start(bf16[912,256]{1,0:T(8,128)(2,1)S(1)} %get-tuple-element.21.refs_2_), channel_id=1, source_target_pairs={{0,16},{16,32},{32,48},{48,64},{64,80},{80,96},{96,112},{112,0},{1... | collective-permute-start | bytes 1400840 | tf_op jit(solution)/shard_map/ppermute | solution.py:276
  102.1 15.0 %collective-permute-start.15 = (bf16[912,256]{1,0:T(8,128)(2,1)}, bf16[912,256]{1,0:T(8,128)(2,1)}, u32[]{:S(2)}, u32[]{:S(2)}) collective-permute-start(bf16[912,256]{1,0:T(8,128)(2,1)} %get-tuple-element.24.refs_2_), channel_id=1, source_target_pairs={{0,16},{16,32},{32,48},{48,64},{64,80},{80,96},{96,112},{112,0},{1... | collective-permute-start | bytes 1400840 | tf_op jit(solution)/shard_map/ppermute | solution.py:276
  102.2 14.9 %collective-permute-start.16 = (bf16[912,256]{1,0:T(8,128)(2,1)}, bf16[912,256]{1,0:T(8,128)(2,1)}, u32[]{:S(2)}, u32[]{:S(2)}) collective-permute-start(bf16[912,256]{1,0:T(8,128)(2,1)} %get-tuple-element.27), channel_id=1, source_target_pairs={{0,112},{16,0},{32,16},{48,32},{64,48},{80,64},{96,80},{112,96},{1... | collective-permute-start | bytes 1400840 | tf_op jit(solution)/shard_map/ppermute | solution.py:276
  105.5 20.2 %collective-permute-start.23 = (f32[16,256]{1,0:T(8,128)S(1)}, f32[16,256]{1,0:T(8,128)S(1)}, u32[]{:S(2)}, u32[]{:S(2)}) collective-permute-start(f32[16,256]{1,0:T(8,128)S(1)} %reshape.38.refs_0_), channel_id=1, source_target_pairs={{0,128},{16,144},{32,160},{48,176},{64,192},{80,208},{96,224},{112... | collective-permute-start | bytes 49160 | tf_op jit(solution)/shard_map/ppermute | solution.py:259
  112.2 20.3 %collective-permute-start.13 = (bf16[912,256]{1,0:T(8,128)(2,1)}, bf16[912,256]{1,0:T(8,128)(2,1)}, u32[]{:S(2)}, u32[]{:S(2)}) collective-permute-start(bf16[912,256]{1,0:T(8,128)(2,1)} %get-tuple-element.25.refs_2_), channel_id=1, source_target_pairs={{0,16},{16,32},{32,48},{48,64},{64,80},{80,96},{96,112},{112,0},{1... | collective-permute-start | bytes 1400840 | tf_op jit(solution)/shard_map/ppermute | solution.py:276
  112.2 20.2 %collective-permute-start.14 = (bf16[912,256]{1,0:T(8,128)(2,1)}, bf16[912,256]{1,0:T(8,128)(2,1)}, u32[]{:S(2)}, u32[]{:S(2)}) collective-permute-start(bf16[912,256]{1,0:T(8,128)(2,1)} %get-tuple-element.26), channel_id=1, source_target_pairs={{0,112},{16,0},{32,16},{48,32},{64,48},{80,64},{96,80},{112,96},{1... | collective-permute-start | bytes 1400840 | tf_op jit(solution)/shard_map/ppermute | solution.py:276
  122.4 18.7 %collective-permute-start.19 = (bf16[912,256]{1,0:T(8,128)(2,1)}, bf16[912,256]{1,0:T(8,128)(2,1)S(1)}, u32[]{:S(2)}, u32[]{:S(2)}) collective-permute-start(bf16[912,256]{1,0:T(8,128)(2,1)} %get-tuple-element.28.refs_2_), channel_id=1, source_target_pairs={{0,16},{16,32},{32,48},{48,64},{64,80},{80,96},{96,112},{112,0},{1... | collective-permute-start | bytes 1400840 | tf_op jit(solution)/shard_map/ppermute | solution.py:276
  122.5 18.6 %collective-permute-start.20 = (bf16[912,256]{1,0:T(8,128)(2,1)}, bf16[912,256]{1,0:T(8,128)(2,1)}, u32[]{:S(2)}, u32[]{:S(2)}) collective-permute-start(bf16[912,256]{1,0:T(8,128)(2,1)} %get-tuple-element.31), channel_id=1, source_target_pairs={{0,112},{16,0},{32,16},{48,32},{64,48},{80,64},{96,80},{112,96},{1... | collective-permute-start | bytes 1400840 | tf_op jit(solution)/shard_map/ppermute | solution.py:276
  126.6 23.2 %all-to-all-start.3 = ((f32[16,32,256]{2,1,0:T(8,128)}), f32[16,32,256]{2,1,0:T(8,128)}, u32[]{:S(2)}, u32[]{:S(2)}) async-start(f32[16,32,256]{2,1,0:T(8,128)} %broadcast_in_dim.5), calls=%async_computation.3 | async-start | bytes 1048576 | tf_op jit(solution)/shard_map/all_to_all | solution.py:262
  137.8 15.1 %collective-permute-start.17 = (bf16[912,256]{1,0:T(8,128)(2,1)}, bf16[912,256]{1,0:T(8,128)(2,1)}, u32[]{:S(2)}, u32[]{:S(2)}) collective-permute-start(bf16[912,256]{1,0:T(8,128)(2,1)} %get-tuple-element.29.refs_2_), channel_id=1, source_target_pairs={{0,16},{16,32},{32,48},{48,64},{64,80},{80,96},{96,112},{112,0},{1... | collective-permute-start | bytes 1400840 | tf_op jit(solution)/shard_map/ppermute | solution.py:276
  137.9 13.0 %copy-start.3 = (f32[8,4096]{1,0:T(8,128)S(1)}, f32[8,4096]{1,0:T(8,128)}, u32[]{:S(2)}) copy-start(f32[8,4096]{1,0:T(8,128)} %param.11) | copy-start | bytes 393220
  137.9 15.0 %collective-permute-start.18 = (bf16[912,256]{1,0:T(8,128)(2,1)}, bf16[912,256]{1,0:T(8,128)(2,1)}, u32[]{:S(2)}, u32[]{:S(2)}) collective-permute-start(bf16[912,256]{1,0:T(8,128)(2,1)} %get-tuple-element.30), channel_id=1, source_target_pairs={{0,112},{16,0},{32,16},{48,32},{64,48},{80,64},{96,80},{112,96},{1... | collective-permute-start | bytes 1400840 | tf_op jit(solution)/shard_map/ppermute | solution.py:276
  146.3 15.8 %collective-permute-start.21 = (bf16[912,256]{1,0:T(8,128)(2,1)}, bf16[912,256]{1,0:T(8,128)(2,1)}, u32[]{:S(2)}, u32[]{:S(2)}) collective-permute-start(bf16[912,256]{1,0:T(8,128)(2,1)} %get-tuple-element.32), channel_id=1, source_target_pairs={{0,16},{16,32},{32,48},{48,64},{64,80},{80,96},{96,112},{112,0},{1... | collective-permute-start | bytes 1400840 | tf_op jit(solution)/shard_map/ppermute | solution.py:276
  146.4 15.8 %collective-permute-start.22 = (bf16[912,256]{1,0:T(8,128)(2,1)}, bf16[912,256]{1,0:T(8,128)(2,1)}, u32[]{:S(2)}, u32[]{:S(2)}) collective-permute-start(bf16[912,256]{1,0:T(8,128)(2,1)} %get-tuple-element.33), channel_id=1, source_target_pairs={{0,112},{16,0},{32,16},{48,32},{64,48},{80,64},{96,80},{112,96},{1... | collective-permute-start | bytes 1400840 | tf_op jit(solution)/shard_map/ppermute | solution.py:276

commit v3 on v1

--- a/solution.py
+++ b/solution.py
@@ -238,9 +238,10 @@
         precision=lax.Precision.HIGHEST,
     )
     devs_t, devs_d = XL * Y * C, XH * Z
-    cols = proj_rank * proj_rank // devs_t
-    part = part.reshape(ex_dev, devs_t, cols).transpose(1, 0, 2)
-    summed = lax.all_to_all(part, "tensor", 0, 0, tiled=True).sum(axis=0)
+    cols = proj_rank * proj_rank // PIECES
+    planes_yc = [list(range(h * PIECES, (h + 1) * PIECES)) for h in range(XL)]
+    part = part.reshape(ex_dev, PIECES, cols).transpose(1, 0, 2)
+    summed = lax.all_to_all(part, "tensor", 0, 0, axis_index_groups=planes_yc, tiled=True).sum(axis=0)
 
     groups = ((4, 3, -3), (2, -2, 1, -1))
     acts = {}
@@ -281,6 +282,7 @@
     back = finish(jnp.stack([(t // C) % Y, t % C]).astype(jnp.int32), own_act, w_down, w_far, came[5], came[6])
     back_grad = back.reshape(ex_dev, seq_len, ff_dev)
 
+    features = features.reshape(XL, PIECES, devs_d * ex_dev, cols).sum(axis=0)
     features = features.transpose(1, 0, 2).reshape(devs_d * ex_dev, proj_rank * proj_rank)
     score_scale = 1.0 / (proj_rank * math.sqrt(seq_len))
     scores = jnp.dot(features, queries.T, precision=lax.Precision.HIGHEST) * score_scale

time: 166 us -> 165 us (level)
  other arithmetic: 5.08 us -> 7.23 us
  waiting for transfers between devices: 39.3 us -> 37.4 us
    ppermute x7, waiting for transfers between devices: 13.2 us -> 9.17 us  [per_device(): lax.ppermute(right, 'dp', Z_PERM[1])]
    reduce_sum x1 -> x2, other arithmetic: 0.03 us -> 2.17 us  [the longest x1 2.15 us: per_device(): features = features.reshape(XL, PIECES, devs_d * ex_dev, cols).sum(axis=0)]
    ppermute x7, starting transfers between devices: 3.13 us -> 1.25 us  [per_device(): lax.ppermute(right, 'dp', Z_PERM[1])]
    ppermute x7, waiting for transfers between devices: 0.02 us -> 1.75 us  [per_device(): lax.ppermute(left, 'dp', Z_PERM[-1])]
  transfers between devices with their start and end apart: 27 -> 27, of which waited for: 10 -> 10; matrix products, arithmetic and copies ran while one was open for 9% -> 11% of each run, Pallas kernels for 24% -> 24%
where the time goes in v3:
time: 165 us; the launch traced here: 164 us
  starting transfers between devices  47.6 us (29%)
  Pallas kernels  42.8 us (26%)
  waiting for transfers between devices  37.4 us (23%)
  blocking collectives  14.6 us (9%)
  other arithmetic  7.23 us (4%)
  local copies, waits for them, and re-layouts  7.03 us (4%)
  matrix products  6.55 us (4%)
    pallas_call x7, Pallas kernels, stage(): pl.pallas_call(functools.partial(stage_kernel, at_r, at_l, part_r, len(ca...  34.8 us
    ppermute x7, starting transfers between devices, per_device(): lax.ppermute(left, 'dp', Z_PERM[-1])  19.9 us
    all_to_all x1, blocking collectives, per_device(): lax.all_to_all(part, 'tensor', 0, 0, axis_index_groups=planes_yc, tiled=T...  14.6 us
    ppermute x6, waiting for transfers between devices, per_device(): lax.ppermute(got, 'tensor', Y_PERM[Y - r])  10.9 us
    all_to_all x1, waiting for transfers between devices, per_device(): lax.all_to_all(columns(own_rows), 'dp', 0, 0, axis_index_groups=rings, ti...  9.81 us
    ppermute x7, waiting for transfers between devices, per_device(): lax.ppermute(right, 'dp', Z_PERM[1])  9.17 us
    all_to_all x1, starting transfers between devices, per_device(): lax.all_to_all(columns(own_rows), 'dp', 0, 0, axis_index_groups=rings, ti...  8.47 us
    ppermute x6, starting transfers between devices, per_device(): lax.ppermute(got, 'tensor', Y_PERM[Y - r])  6.69 us
  transfers between devices with their start and end apart: 27, of which 10 were waited for; matrix products, arithmetic and copies ran while one was open for 11% of the time, Pallas kernels for 24%

profile of v3, /device:TPU:6, one launch (start us, length us, event | category | flops | bytes accessed | tf_op | source)
XLA Modules:
  0.0 164.1 jit_solution(354302991961580364)
XLA Ops:
  0.7 1.2 constant_dynamic-slice_fusion.2
  1.9 0.2 copy.16
  2.2 0.2 copy_bitcast_fusion
  2.3 0.9 maximum_bitcast_fusion
  3.2 8.5 %all-to-all-start = ((bf16[8,32,1024]{2,1,0:T(8,128)(2,1)}), bf16[8,32,1024]{2,1,0:T(8,128)(2,1)S(1)}, u32[]{:S(2)}, u32[]{:S(2)}) async-start(bf16[8,32,1024]{2,1,0:T(8,128)(2,1)} %maximum_bitcast_fusion), calls=%async_computation | async-start | bytes 1048576 | tf_op jit(solution)/shard_map/all_to_all | solution.py:230
  11.7 1.5 collective-permute-start
  13.1 1.6 fusion.2
  14.8 3.6 %fusion = f32[2,128,64]{1,2,0:T(8,128)S(1)} fusion(bf16[2,128,8192]{2,1,0:T(8,128)(2,1)} %param.7, bf16[8192,64]{0,1:T(8,128)(2,1)S(1)} %copy-done), kind=kOutput, calls=%fused_computation.2 | convolution fusion | flops 268435456 | bytes 5308416 | tf_op jit(solution)/shard_map/dot_general | solution.py:233
  18.4 0.2 fusion.4
  18.6 0.1 reshape.40
  18.7 0.6 copy.20
  19.3 9.8 %all-to-all-done.planes = bf16[8,32,1024]{2,1,0:T(8,128)(2,1)S(1)} async-done(((bf16[8,32,1024]{2,1,0:T(8,128)(2,1)}), bf16[8,32,1024]{2,1,0:T(8,128)(2,1)S(1)}, u32[]{:S(2)}, u32[]{:S(2)}) %all-to-all-start) | async-done | bytes 524320 | tf_op jit(solution)/shard_map/all_to_all | solution.py:230
  29.1 0.8 copy-done.2
  29.9 1.9 %shard_map.77 = (bf16[3,32,1024]{2,1,0:T(8,128)(2,1)}, bf16[4,32,1024]{2,1,0:T(8,128)(2,1)}) custom-call(s32[1]{0:T(128)} %bitcast.3.z, bf16[8,32,1024]{2,1,0:T(8,128)(2,1)} %copy-done.2, f32[8,2,512]{2,1,0:T(2,128)} %bitcast.48), custom_call_target="tpu_custom_call" | custom-call | tf_op jit(solution)/shard_map/pallas_call | solution.py:135
  31.8 3.0 %collective-permute-start.5 = (bf16[3,32,1024]{2,1,0:T(8,128)(2,1)}, bf16[3,32,1024]{2,1,0:T(8,128)(2,1)S(1)}, u32[]{:S(2)}, u32[]{:S(2)}) collective-permute-start(bf16[3,32,1024]{2,1,0:T(8,128)(2,1)} %get-tuple-element.19), channel_id=1, source_target_pairs={{0,6},{1,7},{2,0},{3,1},{4,2},{5,3},{6,4},{7,5},{8,14},{9,15},{10,... | collective-permute-start | bytes 589832 | tf_op jit(solution)/shard_map/ppermute | solution.py:249
  34.8 0.6 collective-permute-start.6
  35.4 1.0 collective-permute-start.7
  36.4 7.3 %collective-permute-done.5 = bf16[3,32,1024]{2,1,0:T(8,128)(2,1)S(1)} collective-permute-done((bf16[3,32,1024]{2,1,0:T(8,128)(2,1)}, bf16[3,32,1024]{2,1,0:T(8,128)(2,1)S(1)}, u32[]{:S(2)}, u32[]{:S(2)}) %collective-permute-start.5) | collective-permute-done | bytes 196640 | tf_op jit(solution)/shard_map/ppermute | solution.py:249
  43.7 0.7 collective-permute-done.6
  44.4 2.9 %collective-permute-done.7 = bf16[3,32,1024]{2,1,0:T(8,128)(2,1)S(1)} collective-permute-done((bf16[3,32,1024]{2,1,0:T(8,128)(2,1)}, bf16[3,32,1024]{2,1,0:T(8,128)(2,1)S(1)}, u32[]{:S(2)}, u32[]{:S(2)}) %collective-permute-start.7) | collective-permute-done | bytes 196640 | tf_op jit(solution)/shard_map/ppermute | solution.py:249
  47.3 1.9 %pad_maximum_fusion.1.mine = bf16[4,3,32,1024]{3,2,1,0:T(8,128)(2,1)} fusion(bf16[1,3,32,1024]{3,2,1,0:T(8,128)(2,1)S(1)} %bitcast.56, bf16[1,3,32,1024]{3,2,1,0:T(8,128)(2,1)S(1)} %bitcast.55, bf16[1,3,32,1024]{3,2,1,0:T(8,128)(2,1)S(1)} %bitcast.54, bf16[1,3,32,1024]{3,2,1,0:T(8,128)(2,1)} %bitcast.53), kind=kLoop, calls=%fused_computation.4 | loop fusion | flops 1179648 | bytes 1572864 | tf_op jit(solution)/shard_map/stack | solution.py:249
  49.2 0.1 collective-permute-start.8
  49.3 0.5 collective-permute-start.1
  49.8 0.6 collective-permute-start.2
  50.4 1.0 collective-permute-start.3
  51.4 14.6 %all_to_all.20 = f32[8,2,512]{2,1,0:T(2,128)S(1)} all-to-all(f32[8,2,512]{2,1,0:T(2,128)} %bitcast.49), channel_id=1, replica_groups={{0,1,2,3,4,5,6,7},{8,9,10,11,12,13,14,15},{16,17,18,19,20,21,22,23},{24..., dimensions={0} | all-to-all | bytes 65536 | tf_op jit(solution)/shard_map/all_to_all | solution.py:244
  66.0 0.6 broadcast_in_dim.4
  66.6 3.3 %all-to-all-start.2 = ((f32[8,2,512]{2,1,0:T(2,128)}), f32[8,2,512]{2,1,0:T(2,128)S(1)}, u32[]{:S(2)}, u32[]{:S(2)}) async-start(f32[8,2,512]{2,1,0:T(2,128)} %broadcast_in_dim.4), calls=%async_computation.2 | async-start | bytes 65536 | tf_op jit(solution)/shard_map/all_to_all | solution.py:254
  70.0 2.2 %pad_maximum_fusion.mine = bf16[4,4,32,1024]{3,2,1,0:T(8,128)(2,1)} fusion(bf16[1,4,32,1024]{3,2,1,0:T(8,128)(2,1)} %bitcast.13, bf16[1,4,32,1024]{3,2,1,0:T(8,128)(2,1)S(1)} %bitcast.52, bf16[1,4,32,1024]{3,2,1,0:T(8,128)(2,1)S(1)} %bitcast.51, bf16[1,4,32,1024]{3,2,1,0:T(8,128)(2,1)} %bitcast.50), kind=kLoop, calls=%fused_computation.1 | loop fusion | flops 1572864 | bytes 2097152 | tf_op jit(solution)/shard_map/stack | solution.py:249
  72.1 5.8 %all-to-all-done.2 = f32[8,2,512]{2,1,0:T(2,128)S(1)} async-done(((f32[8,2,512]{2,1,0:T(2,128)}), f32[8,2,512]{2,1,0:T(2,128)S(1)}, u32[]{:S(2)}, u32[]{:S(2)}) %all-to-all-start.2) | async-done | bytes 32800 | tf_op jit(solution)/shard_map/all_to_all | solution.py:254
  78.0 4.0 %shard_map.78 = (bf16[912,256]{1,0:T(8,128)(2,1)S(1)}, bf16[912,256]{1,0:T(8,128)(2,1)S(1)}) custom-call(bf16[4,3,32,1024]{3,2,1,0:T(8,128)(2,1)} %pad_maximum_fusion.1.mine, bf16[4,3,32,1024]{3,2,1,0:T(8,128)(2,1)} %collective-permute-done.8.other, bf16[1792,512]{1,0:T(8,128)(2,1)S(1)} %copy-done.1, bf16[1792,512]{1,0:T(8,128)(2,1)} %collective-permute-done.w_far, ...), custom_call_target="tpu_custom_call" | custom-call | flops 939524096 | bytes 1835008 | tf_op jit(solution)/shard_map/pallas_call | solution.py:157
  81.9 0.6 collective-permute-start.11
  82.5 2.7 %collective-permute-start.12 = (bf16[912,256]{1,0:T(8,128)(2,1)S(1)}, bf16[912,256]{1,0:T(8,128)(2,1)S(1)}, u32[]{:S(2)}, u32[]{:S(2)}) collective-permute-start(bf16[912,256]{1,0:T(8,128)(2,1)S(1)} %get-tuple-element.23), channel_id=1, source_target_pairs={{0,112},{16,0},{32,16},{48,32},{64,48},{80,64},{96,80},{112,96},{1... | collective-permute-start | bytes 1400840 | tf_op jit(solution)/shard_map/ppermute | solution.py:274
  85.2 1.4 collective-permute-start.23
  86.6 4.8 %shard_map.79 = (bf16[912,256]{1,0:T(8,128)(2,1)S(1)}, bf16[912,256]{1,0:T(8,128)(2,1)}) custom-call(bf16[4,3,32,1024]{3,2,1,0:T(8,128)(2,1)} %pad_maximum_fusion.1.mine, bf16[4,3,32,1024]{3,2,1,0:T(8,128)(2,1)} %collective-permute-done.8.other, bf16[1792,512]{1,0:T(8,128)(2,1)S(1)} %copy-done.1, bf16[1792,512]{1,0:T(8,128)(2,1)} %collective-permute-done.w_far, ...), custom_call_target="tpu_custom_call" | custom-call | flops 939524096 | bytes 1835008 | tf_op jit(solution)/shard_map/pallas_call | solution.py:157
  91.4 0.1 collective-permute-start.10
  91.5 3.2 %collective-permute-done.11.refs_0_ = bf16[912,256]{1,0:T(8,128)(2,1)S(1)} collective-permute-done((bf16[912,256]{1,0:T(8,128)(2,1)S(1)}, bf16[912,256]{1,0:T(8,128)(2,1)S(1)}, u32[]{:S(2)}, u32[]{:S(2)}) %collective-permute-start.11) | collective-permute-done | bytes 466976 | tf_op jit(solution)/shard_map/ppermute | solution.py:274
  94.7 1.7 %collective-permute-done.12.refs_1_ = bf16[912,256]{1,0:T(8,128)(2,1)S(1)} collective-permute-done((bf16[912,256]{1,0:T(8,128)(2,1)S(1)}, bf16[912,256]{1,0:T(8,128)(2,1)S(1)}, u32[]{:S(2)}, u32[]{:S(2)}) %collective-permute-start.12) | collective-permute-done | bytes 466976 | tf_op jit(solution)/shard_map/ppermute | solution.py:274
  96.4 5.2 %shard_map.80 = (bf16[912,256]{1,0:T(8,128)(2,1)}, bf16[912,256]{1,0:T(8,128)(2,1)}) custom-call(bf16[4,3,32,1024]{3,2,1,0:T(8,128)(2,1)} %pad_maximum_fusion.1.mine, bf16[4,3,32,1024]{3,2,1,0:T(8,128)(2,1)} %collective-permute-done.8.other, bf16[1792,512]{1,0:T(8,128)(2,1)S(1)} %copy-done.1, bf16[1792,512]{1,0:T(8,128)(2,1)} %collective-permute-done.w_far, ...), custom_call_target="tpu_custom_call" | custom-call | flops 939524096 | bytes 1835008 | tf_op jit(solution)/shard_map/pallas_call | solution.py:157
  101.6 0.3 collective-permute-start.15
  101.9 3.5 %collective-permute-start.16 = (bf16[912,256]{1,0:T(8,128)(2,1)}, bf16[912,256]{1,0:T(8,128)(2,1)}, u32[]{:S(2)}, u32[]{:S(2)}) collective-permute-start(bf16[912,256]{1,0:T(8,128)(2,1)} %get-tuple-element.27), channel_id=1, source_target_pairs={{0,112},{16,0},{32,16},{48,32},{64,48},{80,64},{96,80},{112,96},{1... | collective-permute-start | bytes 1400840 | tf_op jit(solution)/shard_map/ppermute | solution.py:274
  105.5 1.1 broadcast_in_dim.5
  106.6 4.9 %all-to-all-start.3 = ((f32[16,32,512]{2,1,0:T(8,128)}), f32[16,32,512]{2,1,0:T(8,128)}, u32[]{:S(2)}, u32[]{:S(2)}) async-start(f32[16,32,512]{2,1,0:T(8,128)} %broadcast_in_dim.5), calls=%async_computation.3 | async-start | bytes 2097152 | tf_op jit(solution)/shard_map/all_to_all | solution.py:260
  111.5 5.3 %shard_map.81 = (bf16[912,256]{1,0:T(8,128)(2,1)}, bf16[912,256]{1,0:T(8,128)(2,1)}) custom-call(bf16[4,4,32,1024]{3,2,1,0:T(8,128)(2,1)} %pad_maximum_fusion.mine, bf16[4,4,32,1024]{3,2,1,0:T(8,128)(2,1)} %collective-permute-done.4.other, bf16[1792,512]{1,0:T(8,128)(2,1)S(1)} %copy-done.1, bf16[1792,512]{1,0:T(8,128)(2,1)} %collective-permute-done.w_far, ...), custom_call_target="tpu_custom_call" | custom-call | flops 939524096 | bytes 1835008 | tf_op jit(solution)/shard_map/pallas_call | solution.py:157
  116.8 0.1 collective-permute-start.13
  116.9 3.2 %collective-permute-start.14 = (bf16[912,256]{1,0:T(8,128)(2,1)}, bf16[912,256]{1,0:T(8,128)(2,1)}, u32[]{:S(2)}, u32[]{:S(2)}) collective-permute-start(bf16[912,256]{1,0:T(8,128)(2,1)} %get-tuple-element.26), channel_id=1, source_target_pairs={{0,112},{16,0},{32,16},{48,32},{64,48},{80,64},{96,80},{112,96},{1... | collective-permute-start | bytes 1400840 | tf_op jit(solution)/shard_map/ppermute | solution.py:274
  120.2 5.3 %shard_map.82 = (bf16[912,256]{1,0:T(8,128)(2,1)}, bf16[912,256]{1,0:T(8,128)(2,1)}) custom-call(bf16[4,4,32,1024]{3,2,1,0:T(8,128)(2,1)} %pad_maximum_fusion.mine, bf16[4,4,32,1024]{3,2,1,0:T(8,128)(2,1)} %collective-permute-done.4.other, bf16[1792,512]{1,0:T(8,128)(2,1)S(1)} %copy-done.1, bf16[1792,512]{1,0:T(8,128)(2,1)} %collective-permute-done.w_far, ...), custom_call_target="tpu_custom_call" | custom-call | flops 939524096 | bytes 1835008 | tf_op jit(solution)/shard_map/pallas_call | solution.py:157
  125.4 0.1 collective-permute-start.19
  125.5 3.2 %collective-permute-start.20 = (bf16[912,256]{1,0:T(8,128)(2,1)}, bf16[912,256]{1,0:T(8,128)(2,1)}, u32[]{:S(2)}, u32[]{:S(2)}) collective-permute-start(bf16[912,256]{1,0:T(8,128)(2,1)} %get-tuple-element.31), channel_id=1, source_target_pairs={{0,112},{16,0},{32,16},{48,32},{64,48},{80,64},{96,80},{112,96},{1... | collective-permute-start | bytes 1400840 | tf_op jit(solution)/shard_map/ppermute | solution.py:274
  128.8 1.1 constant_dynamic-slice_fusion.4
  129.8 2.2 %collective-permute-done.13.refs_0_ = bf16[912,256]{1,0:T(8,128)(2,1)} collective-permute-done((bf16[912,256]{1,0:T(8,128)(2,1)}, bf16[912,256]{1,0:T(8,128)(2,1)}, u32[]{:S(2)}, u32[]{:S(2)}) %collective-permute-start.13) | collective-permute-done | bytes 466976 | tf_op jit(solution)/shard_map/ppermute | solution.py:274
  132.0 5.2 %shard_map.83 = (bf16[912,256]{1,0:T(8,128)(2,1)}, bf16[912,256]{1,0:T(8,128)(2,1)}) custom-call(bf16[4,4,32,1024]{3,2,1,0:T(8,128)(2,1)} %pad_maximum_fusion.mine, bf16[4,4,32,1024]{3,2,1,0:T(8,128)(2,1)} %collective-permute-done.4.other, bf16[1792,512]{1,0:T(8,128)(2,1)S(1)} %copy-done.1, bf16[1792,512]{1,0:T(8,128)(2,1)} %collective-permute-done.w_far, ...), custom_call_target="tpu_custom_call" | custom-call | flops 939524096 | bytes 1835008 | tf_op jit(solution)/shard_map/pallas_call | solution.py:157
  137.2 0.1 collective-permute-start.17
  137.3 3.3 %collective-permute-start.18 = (bf16[912,256]{1,0:T(8,128)(2,1)}, bf16[912,256]{1,0:T(8,128)(2,1)}, u32[]{:S(2)}, u32[]{:S(2)}) collective-permute-start(bf16[912,256]{1,0:T(8,128)(2,1)} %get-tuple-element.30), channel_id=1, source_target_pairs={{0,112},{16,0},{32,16},{48,32},{64,48},{80,64},{96,80},{112,96},{1... | collective-permute-start | bytes 1400840 | tf_op jit(solution)/shard_map/ppermute | solution.py:274
  140.7 1.2 collective-permute-done.19.refs_0_
  141.9 5.1 %shard_map.85 = (bf16[912,256]{1,0:T(8,128)(2,1)}, bf16[912,256]{1,0:T(8,128)(2,1)}) custom-call(bf16[4,4,32,1024]{3,2,1,0:T(8,128)(2,1)} %pad_maximum_fusion.mine, bf16[4,4,32,1024]{3,2,1,0:T(8,128)(2,1)} %collective-permute-done.4.other, bf16[1792,512]{1,0:T(8,128)(2,1)S(1)} %copy-done.1, bf16[1792,512]{1,0:T(8,128)(2,1)} %collective-permute-done.w_far, ...), custom_call_target="tpu_custom_call" | custom-call | flops 939524096 | bytes 1835008 | tf_op jit(solution)/shard_map/pallas_call | solution.py:157
  147.0 0.1 collective-permute-start.21
  147.1 3.7 %collective-permute-start.22 = (bf16[912,256]{1,0:T(8,128)(2,1)}, bf16[912,256]{1,0:T(8,128)(2,1)}, u32[]{:S(2)}, u32[]{:S(2)}) collective-permute-start(bf16[912,256]{1,0:T(8,128)(2,1)} %get-tuple-element.33), channel_id=1, source_target_pairs={{0,112},{16,0},{32,16},{48,32},{64,48},{80,64},{96,80},{112,96},{1... | collective-permute-start | bytes 1400840 | tf_op jit(solution)/shard_map/ppermute | solution.py:274
  151.0 2.1 %reduce_sum.19 = f32[8,32,512]{2,1,0:T(8,128)} reduce(f32[2,8,32,512]{3,2,1,0:T(8,128)} %bitcast.19, f32[]{:T(128)} %constant.82.clone.1), dimensions={0}, to_apply=%region_1.2 | reduce | flops 131072 | bytes 1572868 | tf_op jit(solution)/shard_map/reduce_sum | solution.py:285
  153.1 1.1 copy.15
  154.2 1.1 convolution_multiply_fusion
  155.3 3.2 %shard_map.84.before = f32[1792,256]{1,0:T(8,128)S(1)} custom-call(s32[2]{0:T(128)S(1)} %pad_add_fusion.place, bf16[256,1024]{1,0:T(8,128)(2,1)S(1)} %pad_maximum_fusion.2.own, bf16[1792,512]{1,0:T(8,128)(2,1)S(1)} %copy-done.1, bf16[1792,512]{1,0:T(8,128)(2,1)} %collective-permute-done.w_far, bf16[912,256]{1,0:T(8,128)(2,1)} %collective-permute-done.17.right, ...), custom_call_target="tpu_custom_call" | custom-call | flops 939524096 | bytes 1835008 | tf_op jit(solution)/shard_map/pallas_call | solution.py:188
  158.6 2.7 %collective-permute-done.21.right = bf16[912,256]{1,0:T(8,128)(2,1)} collective-permute-done((bf16[912,256]{1,0:T(8,128)(2,1)}, bf16[912,256]{1,0:T(8,128)(2,1)}, u32[]{:S(2)}, u32[]{:S(2)}) %collective-permute-start.21) | collective-permute-done | bytes 466976 | tf_op jit(solution)/shard_map/ppermute | solution.py:274
  161.2 2.9 %shard_map.86 = bf16[256,1792]{1,0:T(8,128)(2,1)} custom-call(s32[2]{0:T(128)S(1)} %pad_add_fusion.place, f32[1792,256]{1,0:T(8,128)S(1)} %shard_map.84.before, bf16[912,256]{1,0:T(8,128)(2,1)} %collective-permute-done.21.right, bf16[912,256]{1,0:T(8,128)(2,1)} %collective-permute-done.22.left), custom_call_target="tpu_custom_call" | custom-call | tf_op jit(solution)/shard_map/pallas_call | solution.py:196
  (33 shorter events, 0.3 us)
Async XLA Ops:
  0.6 14.2 %copy-start = (bf16[8192,64]{0,1:T(8,128)(2,1)S(1)}, bf16[8192,64]{0,1:T(8,128)(2,1)}, u32[]{:S(2)}) copy-start(bf16[8192,64]{0,1:T(8,128)(2,1)} %param.10) | copy-start | bytes 3145732
  0.6 11.0 %copy-start.1 = (bf16[1792,512]{1,0:T(8,128)(2,1)S(1)}, bf16[1792,512]{1,0:T(8,128)(2,1)}, u32[]{:S(2)}) copy-start(bf16[1792,512]{1,0:T(8,128)(2,1)} %w_down.15) | copy-start | bytes 5505028
  3.2 26.0 %all-to-all-start = ((bf16[8,32,1024]{2,1,0:T(8,128)(2,1)}), bf16[8,32,1024]{2,1,0:T(8,128)(2,1)S(1)}, u32[]{:S(2)}, u32[]{:S(2)}) async-start(bf16[8,32,1024]{2,1,0:T(8,128)(2,1)} %maximum_bitcast_fusion), calls=%async_computation | async-start | bytes 1048576 | tf_op jit(solution)/shard_map/all_to_all | solution.py:230
  11.7 66.3 %collective-permute-start = (bf16[1792,512]{1,0:T(8,128)(2,1)S(1)}, bf16[1792,512]{1,0:T(8,128)(2,1)}, u32[]{:S(2)}, u32[]{:S(2)}) collective-permute-start(bf16[1792,512]{1,0:T(8,128)(2,1)S(1)} %copy-done.1), channel_id=1, source_target_pairs={{0,128},{16,144},{32,160},{48,176},{64,192},{80,208},{96,224},{112... | collective-permute-start | bytes 5505032 | tf_op jit(solution)/shard_map/ppermute | solution.py:217
  29.1 0.8 copy-start.2
  31.8 11.9 %collective-permute-start.5 = (bf16[3,32,1024]{2,1,0:T(8,128)(2,1)}, bf16[3,32,1024]{2,1,0:T(8,128)(2,1)S(1)}, u32[]{:S(2)}, u32[]{:S(2)}) collective-permute-start(bf16[3,32,1024]{2,1,0:T(8,128)(2,1)} %get-tuple-element.19), channel_id=1, source_target_pairs={{0,6},{1,7},{2,0},{3,1},{4,2},{5,3},{6,4},{7,5},{8,14},{9,15},{10,... | collective-permute-start | bytes 589832 | tf_op jit(solution)/shard_map/ppermute | solution.py:249
  34.8 9.6 %collective-permute-start.6 = (bf16[3,32,1024]{2,1,0:T(8,128)(2,1)}, bf16[3,32,1024]{2,1,0:T(8,128)(2,1)S(1)}, u32[]{:S(2)}, u32[]{:S(2)}) collective-permute-start(bf16[3,32,1024]{2,1,0:T(8,128)(2,1)} %get-tuple-element.19), channel_id=1, source_target_pairs={{0,4},{1,5},{2,6},{3,7},{4,0},{5,1},{6,2},{7,3},{8,12},{9,13},{10,... | collective-permute-start | bytes 589832 | tf_op jit(solution)/shard_map/ppermute | solution.py:249
  35.4 11.8 %collective-permute-start.7 = (bf16[3,32,1024]{2,1,0:T(8,128)(2,1)}, bf16[3,32,1024]{2,1,0:T(8,128)(2,1)S(1)}, u32[]{:S(2)}, u32[]{:S(2)}) collective-permute-start(bf16[3,32,1024]{2,1,0:T(8,128)(2,1)} %get-tuple-element.19), channel_id=1, source_target_pairs={{0,2},{1,3},{2,4},{3,5},{4,6},{5,7},{6,0},{7,1},{8,10},{9,11},{10,... | collective-permute-start | bytes 589832 | tf_op jit(solution)/shard_map/ppermute | solution.py:249
  49.2 28.8 %collective-permute-start.8 = (bf16[4,3,32,1024]{3,2,1,0:T(8,128)(2,1)}, bf16[4,3,32,1024]{3,2,1,0:T(8,128)(2,1)}, u32[]{:S(2)}, u32[]{:S(2)}) collective-permute-start(bf16[4,3,32,1024]{3,2,1,0:T(8,128)(2,1)} %pad_maximum_fusion.1.mine), channel_id=1, source_target_pairs={{0,1},{1,0},{2,3},{3,2},{4,5},{5,4},{6,7},{7,6},{8,9},{9,8},{10,11... | collective-permute-start | bytes 2359304 | tf_op jit(solution)/shard_map/ppermute | solution.py:250
  49.3 20.7 %collective-permute-start.1 = (bf16[4,32,1024]{2,1,0:T(8,128)(2,1)}, bf16[4,32,1024]{2,1,0:T(8,128)(2,1)S(1)}, u32[]{:S(2)}, u32[]{:S(2)}) collective-permute-start(bf16[4,32,1024]{2,1,0:T(8,128)(2,1)} %get-tuple-element.18), channel_id=1, source_target_pairs={{0,6},{1,7},{2,0},{3,1},{4,2},{5,3},{6,4},{7,5},{8,14},{9,15},{10,... | collective-permute-start | bytes 786440 | tf_op jit(solution)/shard_map/ppermute | solution.py:249
  49.8 20.2 %collective-permute-start.2 = (bf16[4,32,1024]{2,1,0:T(8,128)(2,1)}, bf16[4,32,1024]{2,1,0:T(8,128)(2,1)S(1)}, u32[]{:S(2)}, u32[]{:S(2)}) collective-permute-start(bf16[4,32,1024]{2,1,0:T(8,128)(2,1)} %get-tuple-element.18), channel_id=1, source_target_pairs={{0,4},{1,5},{2,6},{3,7},{4,0},{5,1},{6,2},{7,3},{8,12},{9,13},{10,... | collective-permute-start | bytes 786440 | tf_op jit(solution)/shard_map/ppermute | solution.py:249
  50.4 19.6 %collective-permute-start.3 = (bf16[4,32,1024]{2,1,0:T(8,128)(2,1)}, bf16[4,32,1024]{2,1,0:T(8,128)(2,1)}, u32[]{:S(2)}, u32[]{:S(2)}) collective-permute-start(bf16[4,32,1024]{2,1,0:T(8,128)(2,1)} %get-tuple-element.18), channel_id=1, source_target_pairs={{0,2},{1,3},{2,4},{3,5},{4,6},{5,7},{6,0},{7,1},{8,10},{9,11},{10,... | collective-permute-start | bytes 786440 | tf_op jit(solution)/shard_map/ppermute | solution.py:249
  66.6 11.3 %all-to-all-start.2 = ((f32[8,2,512]{2,1,0:T(2,128)}), f32[8,2,512]{2,1,0:T(2,128)S(1)}, u32[]{:S(2)}, u32[]{:S(2)}) async-start(f32[8,2,512]{2,1,0:T(2,128)} %broadcast_in_dim.4), calls=%async_computation.2 | async-start | bytes 65536 | tf_op jit(solution)/shard_map/all_to_all | solution.py:254
  72.1 39.4 %collective-permute-start.4 = (bf16[4,4,32,1024]{3,2,1,0:T(8,128)(2,1)}, bf16[4,4,32,1024]{3,2,1,0:T(8,128)(2,1)}, u32[]{:S(2)}, u32[]{:S(2)}) collective-permute-start(bf16[4,4,32,1024]{3,2,1,0:T(8,128)(2,1)} %pad_maximum_fusion.mine), channel_id=1, source_target_pairs={{0,1},{1,0},{2,3},{3,2},{4,5},{5,4},{6,7},{7,6},{8,9},{9,8},{10,11... | collective-permute-start | bytes 3145736 | tf_op jit(solution)/shard_map/ppermute | solution.py:250
  81.9 12.7 %collective-permute-start.11 = (bf16[912,256]{1,0:T(8,128)(2,1)S(1)}, bf16[912,256]{1,0:T(8,128)(2,1)S(1)}, u32[]{:S(2)}, u32[]{:S(2)}) collective-permute-start(bf16[912,256]{1,0:T(8,128)(2,1)S(1)} %get-tuple-element.20.refs_0_), channel_id=1, source_target_pairs={{0,16},{16,32},{32,48},{48,64},{64,80},{80,96},{96,112},{112,0},{1... | collective-permute-start | bytes 1400840 | tf_op jit(solution)/shard_map/ppermute | solution.py:274
  82.5 13.9 %collective-permute-start.12 = (bf16[912,256]{1,0:T(8,128)(2,1)S(1)}, bf16[912,256]{1,0:T(8,128)(2,1)S(1)}, u32[]{:S(2)}, u32[]{:S(2)}) collective-permute-start(bf16[912,256]{1,0:T(8,128)(2,1)S(1)} %get-tuple-element.23), channel_id=1, source_target_pairs={{0,112},{16,0},{32,16},{48,32},{64,48},{80,64},{96,80},{112,96},{1... | collective-permute-start | bytes 1400840 | tf_op jit(solution)/shard_map/ppermute | solution.py:274
  85.2 16.7 %collective-permute-start.23 = (f32[16,512]{1,0:T(8,128)S(1)}, f32[16,512]{1,0:T(8,128)S(1)}, u32[]{:S(2)}, u32[]{:S(2)}) collective-permute-start(f32[16,512]{1,0:T(8,128)S(1)} %reshape.41.refs_0_), channel_id=1, source_target_pairs={{0,128},{16,144},{32,160},{48,176},{64,192},{80,208},{96,224},{112... | collective-permute-start | bytes 98312 | tf_op jit(solution)/shard_map/ppermute | solution.py:257
  91.4 20.1 %collective-permute-start.10 = (bf16[912,256]{1,0:T(8,128)(2,1)}, bf16[912,256]{1,0:T(8,128)(2,1)}, u32[]{:S(2)}, u32[]{:S(2)}) collective-permute-start(bf16[912,256]{1,0:T(8,128)(2,1)} %get-tuple-element.22), channel_id=1, source_target_pairs={{0,112},{16,0},{32,16},{48,32},{64,48},{80,64},{96,80},{112,96},{1... | collective-permute-start | bytes 1400840 | tf_op jit(solution)/shard_map/ppermute | solution.py:274
  94.6 16.9 %collective-permute-start.9 = (bf16[912,256]{1,0:T(8,128)(2,1)S(1)}, bf16[912,256]{1,0:T(8,128)(2,1)}, u32[]{:S(2)}, u32[]{:S(2)}) collective-permute-start(bf16[912,256]{1,0:T(8,128)(2,1)S(1)} %get-tuple-element.21.refs_2_), channel_id=1, source_target_pairs={{0,16},{16,32},{32,48},{48,64},{64,80},{80,96},{96,112},{112,0},{1... | collective-permute-start | bytes 1400840 | tf_op jit(solution)/shard_map/ppermute | solution.py:274
  101.6 18.6 %collective-permute-start.15 = (bf16[912,256]{1,0:T(8,128)(2,1)}, bf16[912,256]{1,0:T(8,128)(2,1)}, u32[]{:S(2)}, u32[]{:S(2)}) collective-permute-start(bf16[912,256]{1,0:T(8,128)(2,1)} %get-tuple-element.24.refs_2_), channel_id=1, source_target_pairs={{0,16},{16,32},{32,48},{48,64},{64,80},{80,96},{96,112},{112,0},{1... | collective-permute-start | bytes 1400840 | tf_op jit(solution)/shard_map/ppermute | solution.py:274
  101.9 18.3 %collective-permute-start.16 = (bf16[912,256]{1,0:T(8,128)(2,1)}, bf16[912,256]{1,0:T(8,128)(2,1)}, u32[]{:S(2)}, u32[]{:S(2)}) collective-permute-start(bf16[912,256]{1,0:T(8,128)(2,1)} %get-tuple-element.27), channel_id=1, source_target_pairs={{0,112},{16,0},{32,16},{48,32},{64,48},{80,64},{96,80},{112,96},{1... | collective-permute-start | bytes 1400840 | tf_op jit(solution)/shard_map/ppermute | solution.py:274
  106.6 44.4 %all-to-all-start.3 = ((f32[16,32,512]{2,1,0:T(8,128)}), f32[16,32,512]{2,1,0:T(8,128)}, u32[]{:S(2)}, u32[]{:S(2)}) async-start(f32[16,32,512]{2,1,0:T(8,128)} %broadcast_in_dim.5), calls=%async_computation.3 | async-start | bytes 2097152 | tf_op jit(solution)/shard_map/all_to_all | solution.py:260
  116.8 15.1 %collective-permute-start.13 = (bf16[912,256]{1,0:T(8,128)(2,1)}, bf16[912,256]{1,0:T(8,128)(2,1)}, u32[]{:S(2)}, u32[]{:S(2)}) collective-permute-start(bf16[912,256]{1,0:T(8,128)(2,1)} %get-tuple-element.25.refs_2_), channel_id=1, source_target_pairs={{0,16},{16,32},{32,48},{48,64},{64,80},{80,96},{96,112},{112,0},{1... | collective-permute-start | bytes 1400840 | tf_op jit(solution)/shard_map/ppermute | solution.py:274
  116.9 15.1 %collective-permute-start.14 = (bf16[912,256]{1,0:T(8,128)(2,1)}, bf16[912,256]{1,0:T(8,128)(2,1)}, u32[]{:S(2)}, u32[]{:S(2)}) collective-permute-start(bf16[912,256]{1,0:T(8,128)(2,1)} %get-tuple-element.26), channel_id=1, source_target_pairs={{0,112},{16,0},{32,16},{48,32},{64,48},{80,64},{96,80},{112,96},{1... | collective-permute-start | bytes 1400840 | tf_op jit(solution)/shard_map/ppermute | solution.py:274
  125.4 16.4 %collective-permute-start.19 = (bf16[912,256]{1,0:T(8,128)(2,1)}, bf16[912,256]{1,0:T(8,128)(2,1)S(1)}, u32[]{:S(2)}, u32[]{:S(2)}) collective-permute-start(bf16[912,256]{1,0:T(8,128)(2,1)} %get-tuple-element.28.refs_2_), channel_id=1, source_target_pairs={{0,16},{16,32},{32,48},{48,64},{64,80},{80,96},{96,112},{112,0},{1... | collective-permute-start | bytes 1400840 | tf_op jit(solution)/shard_map/ppermute | solution.py:274
  125.5 16.4 %collective-permute-start.20 = (bf16[912,256]{1,0:T(8,128)(2,1)}, bf16[912,256]{1,0:T(8,128)(2,1)}, u32[]{:S(2)}, u32[]{:S(2)}) collective-permute-start(bf16[912,256]{1,0:T(8,128)(2,1)} %get-tuple-element.31), channel_id=1, source_target_pairs={{0,112},{16,0},{32,16},{48,32},{64,48},{80,64},{96,80},{112,96},{1... | collective-permute-start | bytes 1400840 | tf_op jit(solution)/shard_map/ppermute | solution.py:274
  137.2 18.1 %collective-permute-start.17 = (bf16[912,256]{1,0:T(8,128)(2,1)}, bf16[912,256]{1,0:T(8,128)(2,1)}, u32[]{:S(2)}, u32[]{:S(2)}) collective-permute-start(bf16[912,256]{1,0:T(8,128)(2,1)} %get-tuple-element.29.refs_2_), channel_id=1, source_target_pairs={{0,16},{16,32},{32,48},{48,64},{64,80},{80,96},{96,112},{112,0},{1... | collective-permute-start | bytes 1400840 | tf_op jit(solution)/shard_map/ppermute | solution.py:274
  137.3 16.9 %copy-start.3 = (f32[8,4096]{1,0:T(8,128)S(1)}, f32[8,4096]{1,0:T(8,128)}, u32[]{:S(2)}) copy-start(f32[8,4096]{1,0:T(8,128)} %param.11) | copy-start | bytes 393220
  137.3 18.0 %collective-permute-start.18 = (bf16[912,256]{1,0:T(8,128)(2,1)}, bf16[912,256]{1,0:T(8,128)(2,1)}, u32[]{:S(2)}, u32[]{:S(2)}) collective-permute-start(bf16[912,256]{1,0:T(8,128)(2,1)} %get-tuple-element.30), channel_id=1, source_target_pairs={{0,112},{16,0},{32,16},{48,32},{64,48},{80,64},{96,80},{112,96},{1... | collective-permute-start | bytes 1400840 | tf_op jit(solution)/shard_map/ppermute | solution.py:274
  147.0 14.2 %collective-permute-start.21 = (bf16[912,256]{1,0:T(8,128)(2,1)}, bf16[912,256]{1,0:T(8,128)(2,1)}, u32[]{:S(2)}, u32[]{:S(2)}) collective-permute-start(bf16[912,256]{1,0:T(8,128)(2,1)} %get-tuple-element.32), channel_id=1, source_target_pairs={{0,16},{16,32},{32,48},{48,64},{64,80},{80,96},{96,112},{112,0},{1... | collective-permute-start | bytes 1400840 | tf_op jit(solution)/shard_map/ppermute | solution.py:274
  147.1 14.1 %collective-permute-start.22 = (bf16[912,256]{1,0:T(8,128)(2,1)}, bf16[912,256]{1,0:T(8,128)(2,1)}, u32[]{:S(2)}, u32[]{:S(2)}) collective-permute-start(bf16[912,256]{1,0:T(8,128)(2,1)} %get-tuple-element.33), channel_id=1, source_target_pairs={{0,112},{16,0},{32,16},{48,32},{64,48},{80,64},{96,80},{112,96},{1... | collective-permute-start | bytes 1400840 | tf_op jit(solution)/shard_map/ppermute | solution.py:274
